TPU v7x, 256 devices: a whole 4x4x8 slice. The times are simulated.
256 devices in a mesh: pair: 2 (over core), wide: 32 (over y, x, z_lo), rep: 4 (over z_hi).
Axes of the slice: x: 4, y: 4, z: 8 (z_hi: 4, z_lo: 2; z = z_hi * 2 + z_lo), core: 2. Of those that a mesh axis runs over, the one named last changes fastest.
Arguments:
- tokens: bfloat16 [32768, 2560], P(('pair', 'wide', 'rep')), may hold values from -6 to 6
- out_grad: bfloat16 [32768, 2560], P(('pair', 'wide', 'rep')), may hold values from -1.5 to 1.5
- expert_ids: int32 [32768, 6], P(('pair', 'wide', 'rep')), may hold values from 0 to 159, all different within a row; in each aligned block of 128 rows (0 to 127, 128 to 255, ...) at most 12 rows name the same one
- gate_vals: float32 [32768, 6], P(('pair', 'wide', 'rep')), may hold values from 0.03 to 0.6
- gate_weight: bfloat16 [32, 2560, 768], P('wide', None, 'pair'), may hold values from -0.125 to 0.125
- up_weight: bfloat16 [32, 2560, 768], P('wide', None, 'pair'), may hold values from -0.125 to 0.125
- down_weight: bfloat16 [32, 768, 2560], P('wide', 'pair'), may hold values from -0.21875 to 0.21875
Outputs:
- x_grad: bfloat16 [32768, 2560], P(('pair', 'wide', 'rep'))
- gate_grad: float32 [32, 2560, 768], P('wide', 'rep', 'pair')
- up_grad: float32 [32, 2560, 768], P('wide', 'rep', 'pair')
- down_grad: float32 [32, 768, 2560], P('wide', 'pair', 'rep')
Inputs may be any that keep to these rules, and one draw needn't show every extreme that they name: `expert_ids`: each row names 6 different experts; in the 128 rows of one device no expert is named by more than 12 rows.
All inputs are finite; a program needn't handle non-finite values.
Results may differ from a plain program's by a relative error of at most 0.014.
Values may be sent and summed in bfloat16 or wider, within the bound.
No kernel may reach another device: no remote copies, remote signals or barrier semaphores. Data moves between devices by JAX's collectives and lax.ppermute only.
A program may use at most 192 MiB of HBM per device.

v0:
```python
import jax
import jax.numpy as jnp
from jax import lax
from jax.sharding import PartitionSpec as P

WINDOW = 32
CAP = 12


def slot_tables(expert_ids, gate_vals, window, capacity):
    row_count = expert_ids.shape[0]
    choice_count = expert_ids.shape[1]
    flat_ids = expert_ids.reshape(-1)
    flat_gate = gate_vals.reshape(-1)
    chosen = (flat_ids[:, None] == jnp.arange(window, dtype=jnp.int32)[None, :]).astype(jnp.int32)
    before = jnp.cumsum(chosen, axis=0) - chosen
    position = jnp.sum(before * chosen, axis=1)
    inside = jnp.sum(chosen, axis=1)
    target = jnp.where(inside > 0, flat_ids * capacity + position, -1)
    matches = (jnp.arange(window * capacity, dtype=jnp.int32)[:, None] == target[None, :]).astype(
        jnp.int32
    )
    matches = matches.reshape(window * capacity, row_count, choice_count)
    picked = jnp.sum(matches, axis=2)
    weights = jnp.sum(matches.astype(flat_gate.dtype) * gate_vals[None, :, :], axis=2)
    return (picked, weights)


def silu_parts(preact):
    sigmoid_val = jax.nn.sigmoid(preact)
    return (preact * sigmoid_val, sigmoid_val * (1.0 + preact * (1.0 - sigmoid_val)))


def body(tokens, out_grad, expert_ids, gate_vals, gate_weight, up_weight, down_weight):
    pair_count = lax.axis_size("pair")
    wide_count = lax.axis_size("wide")
    rep_count = lax.axis_size("rep")
    local_experts = gate_weight.shape[0]
    features = tokens.shape[1]
    picked, weights = slot_tables(expert_ids, gate_vals, WINDOW, CAP)
    picked_bf = picked.astype(jnp.bfloat16)
    send_rows = jnp.dot(picked_bf, tokens, preferred_element_type=jnp.float32).astype(jnp.bfloat16)
    slot_scale = jnp.sum(weights, axis=1)
    grad_rows = jnp.dot(picked_bf, out_grad, preferred_element_type=jnp.float32)
    send_grads = (slot_scale[:, None] * grad_rows).astype(jnp.bfloat16)
    send_rows = send_rows.reshape(wide_count, local_experts * CAP, features)
    send_grads = send_grads.reshape(wide_count, local_experts * CAP, features)
    landed = (
        lax.all_to_all(send_rows, "wide", split_axis=0, concat_axis=0, tiled=True),
        lax.all_to_all(send_grads, "wide", split_axis=0, concat_axis=0, tiled=True),
    )
    arrived = (
        lax.all_gather(landed[0], "pair", axis=0, tiled=True),
        lax.all_gather(landed[1], "pair", axis=0, tiled=True),
    )
    expert_in = arrived[0].reshape(-1, local_experts, CAP, features)
    expert_grad = arrived[1].reshape(-1, local_experts, CAP, features)
    gate_pre = jnp.einsum(
        "secd,edf->secf", expert_in, gate_weight, preferred_element_type=jnp.float32
    )
    up_pre = jnp.einsum("secd,edf->secf", expert_in, up_weight, preferred_element_type=jnp.float32)
    silu_val, silu_slope = silu_parts(gate_pre)
    hidden_act = (silu_val * up_pre).astype(jnp.bfloat16)
    act_grad = jnp.einsum(
        "secd,efd->secf", expert_grad, down_weight, preferred_element_type=jnp.float32
    )
    gate_back = (act_grad * up_pre * silu_slope).astype(jnp.bfloat16)
    up_back = (act_grad * silu_val).astype(jnp.bfloat16)
    partial_value = jnp.einsum(
        "secf,edf->secd", gate_back, gate_weight, preferred_element_type=jnp.float32
    ) + jnp.einsum("secf,edf->secd", up_back, up_weight, preferred_element_type=jnp.float32)
    partial_value = partial_value.reshape(pair_count, -1, features)
    summed = lax.psum_scatter(partial_value, "pair", scatter_dimension=0, tiled=True)
    outgoing = summed.astype(jnp.bfloat16).reshape(wide_count, local_experts * CAP, features)
    returned = lax.all_to_all(outgoing, "wide", split_axis=0, concat_axis=0, tiled=True).reshape(
        WINDOW * CAP, features
    )
    x_grad = jnp.einsum(
        "st,sd->td", picked_bf, returned, preferred_element_type=jnp.float32
    ).astype(jnp.bfloat16)
    quarter = features // rep_count
    grad_gate = jnp.einsum(
        "secd,secf->def", expert_in, gate_back, preferred_element_type=jnp.float32
    )
    grad_up = jnp.einsum("secd,secf->def", expert_in, up_back, preferred_element_type=jnp.float32)
    grad_down = jnp.einsum(
        "secd,secf->def", expert_grad, hidden_act, preferred_element_type=jnp.float32
    )
    reduced = lax.psum_scatter(
        jnp.stack([grad_gate, grad_up, grad_down], axis=1)
        .reshape(lax.axis_size("rep") * quarter, -1)
        .astype(jnp.bfloat16),
        "rep",
        scatter_dimension=0,
        tiled=True,
    ).astype(jnp.float32)
    reduced = reduced.reshape(quarter, 3, local_experts, -1)
    gate_grad = jnp.transpose(reduced[:, 0], (1, 0, 2))
    up_grad = jnp.transpose(reduced[:, 1], (1, 0, 2))
    down_grad = jnp.transpose(reduced[:, 2], (1, 2, 0))
    return (x_grad, gate_grad, up_grad, down_grad)


def solution(mesh):
    in_specs = (
        P(("pair", "wide", "rep"), None),
        P(("pair", "wide", "rep"), None),
        P(("pair", "wide", "rep"), None),
        P(("pair", "wide", "rep"), None),
        P("wide", None, "pair"),
        P("wide", None, "pair"),
        P("wide", "pair", None),
    )
    out_specs = (
        P(("pair", "wide", "rep"), None),
        P("wide", "rep", "pair"),
        P("wide", "rep", "pair"),
        P("wide", "pair", "rep"),
    )
    return jax.shard_map(body, mesh=mesh, in_specs=in_specs, out_specs=out_specs, check_vma=False)
```

profile of v0, /device:TPU:33, one launch (start us, length us, event | category | flops | bytes accessed | tf_op | source)
XLA Modules:
  0.0 350.3 jit_solution(14738133832582374781)
XLA Ops:
  7.2 0.0 copy-start
  7.2 0.9 copy.58
  8.1 0.1 eq.44
  8.3 0.1 eq.40
  8.4 1.7 reduce-window.6
  10.2 0.3 slice_reduce_fusion
  10.4 0.1 fusion.35
  10.6 0.2 gt.15
  10.7 0.1 copy.62
  10.8 0.2 reduce_sum.44
  11.0 0.1 copy.61
  11.0 0.7 add_select_fusion
  11.7 0.1 convert_reduce_fusion
  11.9 3.0 convolution_convert_fusion
  14.9 4.0 %reshape.126 = bf16[32,12,2560]{2,1,0:T(8,128)(2,1)} reshape(bf16[384,2560]{1,0:T(8,128)(2,1)} %convolution_convert_fusion) | data formatting | bytes 3932160 | tf_op jit(solution)/shard_map/reshape | solution.py:46
  18.9 8.2 %all-to-all-start.1 = ((bf16[32,12,2560]{2,1,0:T(8,128)(2,1)}), bf16[32,12,2560]{2,1,0:T(8,128)(2,1)}, u32[]{:S(2)}, u32[]{:S(2)}) async-start(bf16[32,12,2560]{2,1,0:T(8,128)(2,1)} %reshape.126), calls=%async_computation.1 | async-start | bytes 5242880 | tf_op jit(solution)/shard_map/all_to_all | solution.py:49
  27.1 0.0 all-gather.5.cloned.1.call-start
  27.2 0.2 fusion.26
  27.4 33.2 %all-to-all-done.1 = bf16[32,12,2560]{2,1,0:T(8,128)(2,1)} async-done(((bf16[32,12,2560]{2,1,0:T(8,128)(2,1)}), bf16[32,12,2560]{2,1,0:T(8,128)(2,1)}, u32[]{:S(2)}, u32[]{:S(2)}) %all-to-all-start.1) | async-done | bytes 1966112 | tf_op jit(solution)/shard_map/all_to_all | solution.py:49
  60.6 4.1 %copy.64 = bf16[32,12,2560]{2,0,1:T(8,128)(2,1)} copy(bf16[32,12,2560]{2,1,0:T(8,128)(2,1)} %all-to-all-done.1) | data formatting | bytes 3932160 | tf_op jit(solution)/shard_map/all_to_all | solution.py:49
  64.7 0.0 all-gather.5.cloned.1.call-update
  64.8 0.0 all-gather.3.cloned.1.call-start
  64.8 1.0 copy-done.4
  65.8 2.0 fusion
  67.8 4.0 %reshape.124 = bf16[32,12,2560]{2,1,0:T(8,128)(2,1)} reshape(bf16[384,2560]{1,0:T(8,128)(2,1)} %fusion) | data formatting | bytes 3932160 | tf_op jit(solution)/shard_map/reshape | solution.py:47
  71.8 37.2 %all_to_all.15 = bf16[32,12,2560]{2,1,0:T(8,128)(2,1)S(1)} all-to-all(bf16[32,12,2560]{2,1,0:T(8,128)(2,1)} %reshape.124), channel_id=1, replica_groups=mesh['pair'=2,'wide'=32,'rep'=4] {'wide'}, dimensions={0} | all-to-all | bytes 3932160 | tf_op jit(solution)/shard_map/all_to_all | solution.py:50
  109.0 2.4 copy.63
  111.4 0.0 all-gather.3.cloned.1.call-update
  111.4 0.2 reduce-scatter.5.cloned.1.call-start
  111.7 0.0 all-gather.5.cloned.1.call-done
  111.7 0.0 copy-start.2
  111.7 5.5 %fusion.22 = f32[64,1,12,384]{3,0,2,1:T(8,128)} fusion(bf16[64,12,2560]{2,0,1:T(8,128)(2,1)} %all-gather.5.cloned.1.call-done, bf16[1,2560,384]{2,1,0:T(8,128)(2,1)S(1)} %copy-done), kind=kOutput, calls=%fused_computation.28 | convolution fusion | flops 1509949440 | bytes 7077888 | tf_op jit(solution)/shard_map/secd,edf->secf/dot_general | solution.py:58
  117.2 3.2 fusion.19
  120.4 12.2 %all-gather.3.cloned.1.call-done = bf16[64,12,2560]{2,0,1:T(8,128)(2,1)} async-done(((bf16[32,12,2560]{2,0,1:T(8,128)(2,1)}), bf16[64,12,2560]{2,0,1:T(8,128)(2,1)}) %all-gather.3.cloned.1.call-update) | async-done | bytes 3932176 | tf_op jit(solution)/shard_map/all_gather | solution.py:54
  132.6 5.8 %fusion.28 = (bf16[64,12,384]{2,0,1:T(8,128)(2,1)S(1)}, bf16[64,1,12,384]{3,0,2,1:T(8,128)(2,1)S(1)}) fusion(f32[64,1,12,384]{3,0,2,1:T(8,128)} %fusion.22, f32[64,1,12,384]{3,0,2,1:T(8,128)} %fusion.19, bf16[64,12,2560]{2,0,1:T(8,128)(2,1)} %all-gather.3.cloned.1.call-done, bf16[1,384,2560]{2,1,0:T(8,128)(2,1)} %param.13), kind=kOutput, calls=%fused_computation.38 | convolution fusion | flops 1513783296 | bytes 9437184 | tf_op jit(solution)/shard_map/secd,efd->secf/dot_general | solution.py:64
  138.5 0.0 copy-start.3
  138.5 2.2 fusion.7
  140.7 2.2 add_bitcast_fusion
  143.0 8.6 %copy.65 = f32[64,1,12,2560]{3,2,0,1:T(8,128)} copy(f32[64,1,12,2560]{3,0,2,1:T(8,128)S(1)} %add_bitcast_fusion) | data formatting | bytes 15728640 | tf_op jit(solution)/shard_map/add | solution.py:69
  151.6 9.4 %reshape.131 = f32[2,384,2560]{2,1,0:T(8,128)} reshape(f32[64,1,12,2560]{3,2,0,1:T(8,128)} %copy.65) | data formatting | bytes 15728640 | tf_op jit(solution)/shard_map/reshape | solution.py:72
  161.0 0.0 reduce-scatter.5.cloned.1.call-update
  161.0 0.3 reduce-scatter.7.cloned.1.call-start
  161.3 4.2 %fusion.5 = bf16[2560,1,1,384]{0,3,2,1:T(8,128)(2,1)S(1)} fusion(bf16[64,12,384]{2,0,1:T(8,128)(2,1)} %copy-done.5, bf16[64,12,2560]{2,0,1:T(8,128)(2,1)} %all-gather.5.cloned.1.call-done), kind=kOutput, calls=%fused_computation.12 | convolution fusion | flops 1510932480 | bytes 6488064 | tf_op jit(solution)/shard_map/secd,secf->def/dot_general | solution.py:85
  165.5 1.7 fusion.6
  167.2 0.3 copy-done.9
  167.6 0.3 copy-done.10
  167.9 0.4 copy-done.11
  168.3 1.8 fusion.4
  170.1 3.1 pad_maximum_fusion
  173.1 9.3 %copy.68 = bf16[2560,1152]{1,0:T(8,128)(2,1)} copy(bf16[2560,1152]{0,1:T(8,128)(2,1)} %bitcast.131) | data formatting | bytes 11796480
  182.5 0.0 reduce-scatter.7.cloned.1.call-update
  182.5 1.8 reduce-scatter.5.cloned.1.call-done
  184.3 2.3 convert_element_type.52
  186.6 2.3 reshape.132
  188.9 7.8 %all-to-all-start.2 = ((bf16[32,12,2560]{2,1,0:T(8,128)(2,1)}), bf16[32,12,2560]{2,1,0:T(8,128)(2,1)}, u32[]{:S(2)}, u32[]{:S(2)}) async-start(bf16[32,12,2560]{2,1,0:T(8,128)(2,1)} %reshape.132), calls=%async_computation.3 | async-start | bytes 5242880 | tf_op jit(solution)/shard_map/all_to_all | solution.py:75
  196.7 128.6 %reduce-scatter.7.cloned.1.call-done = bf16[640,1152]{1,0:T(8,128)(2,1)} async-done(((bf16[2560,1152]{1,0:T(8,128)(2,1)}), bf16[640,1152]{1,0:T(8,128)(2,1)}) %reduce-scatter.7.cloned.1.call-update) | async-done | bytes 1474576
  325.3 2.6 copy.69
  327.8 1.8 convert.22
  329.6 1.1 fusion.41
  330.7 2.5 copy.67
  333.2 1.3 copy.66
  334.5 2.2 slice_bitcast_fusion
  336.7 4.2 %reshape.133 = bf16[384,2560]{1,0:T(8,128)(2,1)} reshape(bf16[32,12,2560]{2,1,0:T(8,128)(2,1)} %all-to-all-done.2) | data formatting | bytes 3932160 | tf_op jit(solution)/shard_map/reshape | solution.py:75
  340.8 2.9 convolution_convert_fusion.1
  (21 shorter events, 0.1 us)
Async XLA Ops:
  7.2 104.5 %copy-start = (bf16[1,2560,384]{2,1,0:T(8,128)(2,1)S(1)}, bf16[1,2560,384]{2,1,0:T(8,128)(2,1)}, u32[]{:S(2)}) copy-start(bf16[1,2560,384]{2,1,0:T(8,128)(2,1)} %param.11) | copy-start | bytes 5898244
  18.9 8.2 %copy-start.6 = (f32[128,6]{0,1:T(8,128)S(1)}, f32[128,6]{0,1:T(8,128)}, u32[]{:S(2)}) copy-start(f32[128,6]{0,1:T(8,128)} %param.10) | copy-start | bytes 9220
  18.9 41.7 %all-to-all-start.1 = ((bf16[32,12,2560]{2,1,0:T(8,128)(2,1)}), bf16[32,12,2560]{2,1,0:T(8,128)(2,1)}, u32[]{:S(2)}, u32[]{:S(2)}) async-start(bf16[32,12,2560]{2,1,0:T(8,128)(2,1)} %reshape.126), calls=%async_computation.1 | async-start | bytes 5242880 | tf_op jit(solution)/shard_map/all_to_all | solution.py:49
  27.1 84.6 %all-gather.5.cloned.1.call-start = ((), (), s32[]{:S(2)}) async-start(), calls=%async_computation.6 | async-start | bytes 5898240 | tf_op jit(solution)/shard_map/all_gather | solution.py:53
  64.7 1.1 copy-start.4
  64.8 67.8 %all-gather.3.cloned.1.call-start = ((), (), s32[]{:S(2)}) async-start(), calls=%async_computation.5 | async-start | bytes 5898240 | tf_op jit(solution)/shard_map/all_gather | solution.py:54
  111.4 72.9 %reduce-scatter.5.cloned.1.call-start = ((), (), s32[]{:S(2)}) async-start(), calls=%async_computation.7 | async-start | bytes 11796480 | tf_op jit(solution)/shard_map/reduce_scatter | solution.py:73
  111.7 5.5 %copy-start.2 = (bf16[1,2560,384]{2,1,0:T(8,128)(2,1)S(1)}, bf16[1,2560,384]{2,1,0:T(8,128)(2,1)}, u32[]{:S(2)}) copy-start(bf16[1,2560,384]{2,1,0:T(8,128)(2,1)} %param.12) | copy-start | bytes 5898244
  111.7 5.5 %copy-start.7 = (bf16[64,12,2560]{2,0,1:T(8,128)(2,1)S(1)}, bf16[64,12,2560]{2,0,1:T(8,128)(2,1)}, u32[]{:S(2)}) copy-start(bf16[64,12,2560]{2,0,1:T(8,128)(2,1)} %all-gather.5.cloned.1.call-done) | copy-start | bytes 11796484
  138.5 2.3 copy-start.5
  138.5 2.3 copy-start.3
  161.0 164.3 %reduce-scatter.7.cloned.1.call-start = ((), (), s32[]{:S(2)}) async-start(), calls=%async_computation.8 | async-start | bytes 7372800
  161.3 4.2 %copy-start.8 = (bf16[64,12,2560]{2,0,1:T(8,128)(2,1)S(1)}, bf16[64,12,2560]{2,0,1:T(8,128)(2,1)}, u32[]{:S(2)}) copy-start(bf16[64,12,2560]{2,0,1:T(8,128)(2,1)} %all-gather.5.cloned.1.call-done) | copy-start | bytes 11796484
  165.5 2.1 copy-start.9
  165.5 2.4 copy-start.10
  165.5 2.8 copy-start.11
  188.9 147.8 %all-to-all-start.2 = ((bf16[32,12,2560]{2,1,0:T(8,128)(2,1)}), bf16[32,12,2560]{2,1,0:T(8,128)(2,1)}, u32[]{:S(2)}, u32[]{:S(2)}) async-start(bf16[32,12,2560]{2,1,0:T(8,128)(2,1)} %reshape.132), calls=%async_computation.3 | async-start | bytes 5242880 | tf_op jit(solution)/shard_map/all_to_all | solution.py:75
  336.7 7.1 %copy-start.1 = (bf16[1,2560,384]{2,1,0:T(8,128)(2,1)S(1)}, bf16[1,2560,384]{2,1,0:T(8,128)(2,1)}, u32[]{:S(2)}) copy-start(bf16[1,2560,384]{2,1,0:T(8,128)(2,1)} %param.11) | copy-start | bytes 5898244
Sparse Core Ops, SparseCore 0:
  64.9 20.2 all-gather.4
  111.6 20.9 all-gather.2
  161.1 23.1 reduce-scatter.4
  186.9 138.3 reduce-scatter.6
where the time goes:
time: 352 us; the launch traced here: 350 us
  waiting for transfers between devices  176 us (50%)
  local copies, waits for them, and re-layouts  61.8 us (18%)
  blocking collectives  37.2 us (11%)
  matrix products  34.7 us (10%)
  starting transfers between devices  16.5 us (5%)
  between operations  14 us (4%)
  other arithmetic  10.1 us (3%)
    unnamed x5, waiting for transfers between devices  129 us
    all_to_all x1, blocking collectives, body(): lax.all_to_all(send_grads, 'wide', split_axis=0, concat_axis=0, tiled=True)  37.2 us
    all_to_all x1, waiting for transfers between devices, body(): lax.all_to_all(send_rows, 'wide', split_axis=0, concat_axis=0, tiled=True)  33.2 us
    unnamed x27, local copies, waits for them, and re-layouts  14.9 us
    all_gather x1, waiting for transfers between devices, body(): lax.all_gather(landed[1], 'pair', axis=0, tiled=True)  12.2 us
    reshape x1, local copies, waits for them, and re-layouts, body(): partial_value = partial_value.reshape(pair_count, -1, features)  9.38 us
    add x1, local copies, waits for them, and re-layouts, body(): jnp.einsum('secf,edf->secd', gate_back, gate_weight, preferred_element_ty...  8.63 us
    all_to_all x1, starting transfers between devices, body(): lax.all_to_all(send_rows, 'wide', split_axis=0, concat_axis=0, tiled=True)  8.17 us
  transfers between devices with their start and end apart: 6, of which 4 were waited for; matrix products, arithmetic and copies ran while one was open for 15% of the time, Pallas kernels for 0%

commit v1 on v0

v1 whole, which is shorter than its diff:
```python
import functools
import jax
import jax.numpy as jnp
from jax import lax
from jax.experimental import pallas as pl
from jax.experimental.pallas import tpu as pltpu
from jax.sharding import PartitionSpec as P

WINDOW = 32
CAP = 12
BF = jnp.bfloat16
F32 = jnp.float32
MIB = 1024 * 1024


def dot(a, b, ca, cb):
    return lax.dot_general(a, b, (((ca,), (cb,)), ((), ())), preferred_element_type=F32)


def call(kernel, grid, in_specs, out_specs, out_shape, args, scratch=(), grant=24):
    spec = pltpu.PrefetchScalarGridSpec(
        num_scalar_prefetch=1,
        grid=grid,
        in_specs=in_specs,
        out_specs=out_specs,
        scratch_shapes=scratch,
    )
    return pl.pallas_call(
        kernel,
        grid_spec=spec,
        out_shape=out_shape,
        compiler_params=pltpu.CompilerParams(
            dimension_semantics=("arbitrary",) * len(grid), vmem_limit_bytes=grant * MIB
        ),
        cost_estimate=pl.CostEstimate(flops=1, bytes_accessed=1, transcendentals=0),
    )(*args)


def block_codes(ids, gates):
    choices, rows = ids.shape
    expert = lax.broadcasted_iota(jnp.int32, (WINDOW, rows), 0)
    chosen = jnp.zeros((WINDOW, rows), F32)
    gate = jnp.zeros((WINDOW, rows), F32)
    for k in range(choices):
        hit = ids[k : k + 1, :] == expert
        chosen = jnp.where(hit, 1.0, chosen)
        gate = jnp.where(hit, gates[k : k + 1, :], gate)
    earlier = (
        lax.broadcasted_iota(jnp.int32, (rows, rows), 0)
        < lax.broadcasted_iota(jnp.int32, (rows, rows), 1)
    ).astype(F32)
    before = dot(chosen.astype(BF), earlier.astype(BF), 1, 0)
    code = jnp.where(chosen > 0.5, before.astype(jnp.int32), -100)
    return code, gate


def pack_kernel(pos, ids_a, ids_b, gv_a, gv_b, tok_a, tok_b, og_a, og_b, out, sel_t, sel, scale):
    @pl.when(pl.program_id(0) == 0)
    def _():
        core = pos[0]
        code_a, gate_a = block_codes(ids_a[...], gv_a[...])
        code_b, gate_b = block_codes(ids_b[...], gv_b[...])
        code = jnp.concatenate([code_a + CAP * core, code_b + CAP * (1 - core)], axis=1)
        gate = jnp.concatenate([gate_a, gate_b], axis=1)
        width = code.shape[1]
        slot = lax.broadcasted_iota(jnp.int32, (WINDOW, 2 * CAP, width), 1)
        hit = code[:, None, :] == slot
        picked = jnp.where(hit, 1.0, 0.0).reshape(WINDOW * 2 * CAP, width).astype(BF)
        weight = jnp.where(hit, gate[:, None, :], 0.0).reshape(WINDOW * 2 * CAP, width)
        sel[...] = picked
        sel_t[...] = picked.T
        scale[...] = jnp.sum(weight, axis=1, keepdims=True)

    shape = (WINDOW, 2 * CAP, out.shape[3])
    both = jnp.concatenate([tok_a[...], tok_b[...]], axis=0)
    out[:, 0] = dot(sel[...], both, 1, 0).reshape(shape).astype(BF)
    both = jnp.concatenate([og_a[...], og_b[...]], axis=0)
    out[:, 1] = (dot(sel[...], both, 1, 0) * scale[...]).reshape(shape).astype(BF)


def turn_kernel(pos, wd, wg, wu, wd_t, wgu, wgu_t):
    hid = wd.shape[0]
    wd_t[...] = wd[...].T
    wgu[:, :hid] = wg[...]
    wgu[:, hid:] = wu[...]
    wgu_t[:hid] = wg[...].T
    wgu_t[hid:] = wu[...].T


def forward_kernel(pos, x_a, x_b, w_a, w_b, x_t, hidden_t, factors):
    xa, xb = x_a[...], x_b[...]
    pre = dot(xa, w_a[0], 1, 0) + dot(xb, w_b[0], 1, 0)
    hid = pre.shape[1] // 2
    gate_pre, up_pre = pre[:, :hid], pre[:, hid:]
    sig = jax.nn.sigmoid(gate_pre)
    silu = gate_pre * sig
    hidden_t[...] = (silu * up_pre).astype(BF).T
    factors[:, :hid] = up_pre * (sig * (1.0 + gate_pre * (1.0 - sig)))
    factors[:, hid:] = silu
    x_t[pos[0]] = xa.T
    x_t[1 - pos[0]] = xb.T


def act_kernel(pos, g_a, g_b, wd_a, wd_b, factors, backs):
    act = dot(g_a[...], wd_a[0], 1, 0) + dot(g_b[...], wd_b[0], 1, 0)
    hid = act.shape[1]
    backs[:, :hid] = (act * factors[:, :hid]).astype(BF)
    backs[:, hid:] = (act * factors[:, hid:]).astype(BF)


def down_kernel(shift, pos, hidden_t, g_a, g_b, *outs):
    def run(g):
        value = dot(hidden_t[...], g[...], 1, 0)
        step = value.shape[0] // len(outs)
        for i, out in enumerate(outs):
            out[...] = value[i * step : (i + 1) * step].astype(out.dtype)

    mine = (lax.rem(pos[1] + shift, 4) // 2) == pos[0]

    @pl.when(mine)
    def _():
        run(g_a)

    @pl.when(jnp.logical_not(mine))
    def _():
        run(g_b)


def gate_up_kernel(pos, x_t, backs, gate_out, up_out):
    value = dot(x_t[...], backs[...], 1, 0)
    hid = gate_out.shape[1]
    gate_out[...] = value[:, :hid].astype(gate_out.dtype)
    up_out[...] = value[:, hid:].astype(up_out.dtype)


def row_send_kernel(pos, backs, wgu, out):
    out[...] = dot(backs[...], wgu[...], 1, 0).astype(out.dtype)


def row_sum_kernel(pos, backs, wgu, got, out):
    value = dot(backs[...], wgu[...], 1, 0)
    out[...] = (value + got[...].astype(F32)).astype(out.dtype)


def token_kernel(pos, sel, rows, own, other):
    value = dot(sel[...], rows[...], 1, 0)
    half = value.shape[0] // 2
    own[...] = value[:half].astype(BF)
    other[...] = value[half:].astype(BF)


def body(tokens, out_grad, expert_ids, gate_vals, gate_weight, up_weight, down_weight):
    count, features = tokens.shape
    half = features // 2
    quarter = features // 4
    hid = gate_weight.shape[2]
    wide = lax.axis_size("wide")
    choices = expert_ids.shape[1]
    total = WINDOW * 2 * CAP
    core = lax.axis_index("pair").astype(jnp.int32)
    rep = lax.axis_index("rep").astype(jnp.int32)
    pos = jnp.stack([core, rep])
    swap = [(0, 1), (1, 0)]
    up = [(i, (i + 1) % 4) for i in range(4)]
    down = [(i, (i + 3) % 4) for i in range(4)]
    sds = jax.ShapeDtypeStruct

    def full(*shape):
        return pl.BlockSpec(shape, lambda *_: (0,) * len(shape))

    ids = expert_ids.T
    gates = gate_vals.T
    ids_b = lax.ppermute(ids, "pair", swap)
    gv_b = lax.ppermute(gates, "pair", swap)
    tok_b = lax.ppermute(tokens, "pair", swap)
    og_b = lax.ppermute(out_grad, "pair", swap)

    def after(place, *values):
        return lax.optimization_barrier((place, *values))[0]

    steps = 5
    wcol = half // steps
    tok_spec = pl.BlockSpec((count, wcol), lambda i, p: (0, p[0] * steps + i))
    out_col = pl.BlockSpec((total, wcol), lambda i, p: (0, i))
    sent, sel_t = call(
        pack_kernel,
        (steps,),
        [full(choices, count)] * 4 + [tok_spec] * 4,
        [
            pl.BlockSpec((wide, 2, 2 * CAP, wcol), lambda i, p: (0, 0, 0, i)),
            full(2 * count, total),
        ],
        [sds((wide, 2, 2 * CAP, half), BF), sds((2 * count, total), BF)],
        (pos, ids, ids_b, gates, gv_b, tokens, tok_b, out_grad, og_b),
        scratch=[pltpu.VMEM((total, 2 * count), BF), pltpu.VMEM((total, 1), F32)],
        grant=56,
    )
    pos = after(pos, sent)
    wg_full = gate_weight.reshape(features, hid)
    wu_full = up_weight.reshape(features, hid)
    wd = down_weight.reshape(hid, features)
    tall = pl.BlockSpec((features // steps, hid), lambda i, p: (i, 0))
    flat = pl.BlockSpec((hid, features // steps), lambda i, p: (0, i))
    wd_t, wgu, wgu_t = call(
        turn_kernel,
        (steps,),
        [flat, tall, tall],
        [
            tall,
            pl.BlockSpec((features // steps, 2 * hid), lambda i, p: (i, 0)),
            pl.BlockSpec((2 * hid, features // steps), lambda i, p: (0, i)),
        ],
        [sds((features, hid), BF), sds((features, 2 * hid), BF), sds((2 * hid, features), BF)],
        (pos, wd, wg_full, wu_full),
    )
    pos = after(pos, wd_t)
    landed = lax.all_to_all(sent, "wide", split_axis=0, concat_axis=0, tiled=True)
    x_own = landed[:, 0].reshape(total, half)
    g_own = landed[:, 1].reshape(total, half)
    x_oth = lax.ppermute(x_own, "pair", swap)

    parts = 3
    prow = total // parts
    wgu = wgu.reshape(2, half, 2 * hid)
    wd_t = wd_t.reshape(2, half, hid)
    rows_in = pl.BlockSpec((prow, half), lambda i, p: (i, 0))
    rows_two = pl.BlockSpec((prow, 2 * hid), lambda i, p: (i, 0))

    def w_own(n):
        return pl.BlockSpec((1, half, n), lambda i, p: (p[0], 0, 0))

    def w_oth(n):
        return pl.BlockSpec((1, half, n), lambda i, p: (1 - p[0], 0, 0))

    x_t, hidden_t, factors = call(
        forward_kernel,
        (parts,),
        [rows_in, rows_in, w_own(2 * hid), w_oth(2 * hid)],
        [
            pl.BlockSpec((2, half, prow), lambda i, p: (0, 0, i)),
            pl.BlockSpec((hid, prow), lambda i, p: (0, i)),
            rows_two,
        ],
        [sds((2, half, total), BF), sds((hid, total), BF), sds((total, 2 * hid), F32)],
        (pos, x_own, x_oth, wgu, wgu),
    )
    x_t = x_t.reshape(features, total)
    pos = after(pos, hidden_t)
    g_oth = lax.ppermute(g_own, "pair", swap)

    def down_part(place, shift, dtype, pieces):
        g_spec = pl.BlockSpec((total, quarter), lambda i, p: (0, lax.rem(p[1] + shift, 2)))
        return call(
            functools.partial(down_kernel, shift),
            (1,),
            [full(hid, total)] + [g_spec] * 2,
            [full(hid // pieces, quarter)] * pieces,
            [sds((hid // pieces, quarter), dtype)] * pieces,
            (place, hidden_t, g_own, g_oth),
        )

    def gate_up_part(place, shift, dtype):
        return call(
            gate_up_kernel,
            (1,),
            [
                pl.BlockSpec((quarter, total), lambda i, p: (lax.rem(p[1] + shift, 4), 0)),
                full(total, 2 * hid),
            ],
            [full(quarter, hid)] * 2,
            [sds((quarter, hid), dtype)] * 2,
            (place, x_t, backs),
        )

    def add(a, b):
        return (a.astype(F32) + b.astype(F32)).astype(BF)

    far = down_part(pos, 2, BF, 2)
    d_far_u = lax.ppermute(far[0], "rep", up)
    d_far_d = lax.ppermute(far[1], "rep", down)
    pos = after(pos, *far)
    nxt = down_part(pos, 1, BF, 2)
    prv = down_part(pos, 3, BF, 2)
    d_near_u = lax.ppermute(nxt[1], "rep", up)
    d_near_d = lax.ppermute(prv[0], "rep", down)
    pos = after(pos, *nxt, *prv)

    backs = call(
        act_kernel,
        (parts,),
        [rows_in, rows_in, w_own(hid), w_oth(hid), rows_two],
        [rows_two],
        [sds((total, 2 * hid), BF)],
        (pos, g_own, g_oth, wd_t, wd_t, factors),
    )[0]
    d_far_u, d_far_d, backs = lax.optimization_barrier((d_far_u, d_far_d, backs))
    d_sum_u = lax.ppermute(add(nxt[0], d_far_u), "rep", up)
    d_sum_d = lax.ppermute(add(prv[1], d_far_d), "rep", down)

    t_own = pl.BlockSpec((2 * hid, half), lambda i, p: (0, p[0]))
    t_oth = pl.BlockSpec((2 * hid, half), lambda i, p: (0, 1 - p[0]))
    row_send = call(
        row_send_kernel,
        (parts,),
        [rows_two, t_oth],
        [rows_in],
        [sds((total, half), BF)],
        (pos, backs, wgu_t),
    )[0]
    row_got = lax.ppermute(row_send, "pair", swap)
    pos = after(pos, row_send)
    g_far, u_far = gate_up_part(pos, 2, BF)
    pos = after(pos, g_far, u_far)
    row_grad = call(
        row_sum_kernel,
        (parts,),
        [rows_two, t_own, rows_in],
        [rows_in],
        [sds((total, half), BF)],
        (pos, backs, wgu_t, row_got),
    )[0]
    row_grad, pos, g_far, u_far, d_near_u, d_near_d, d_sum_u, d_sum_d = lax.optimization_barrier(
        (row_grad, pos, g_far, u_far, d_near_u, d_near_d, d_sum_u, d_sum_d)
    )
    back = lax.all_to_all(
        row_grad.reshape(wide, 2 * CAP, half), "wide", split_axis=0, concat_axis=0, tiled=True
    ).reshape(total, half)
    g_far = lax.ppermute(g_far, "rep", up)
    u_far = lax.ppermute(u_far, "rep", down)
    g_nxt, u_nxt = gate_up_part(pos, 1, BF)
    g_prv, u_prv = gate_up_part(pos, 3, BF)
    u_near = lax.ppermute(u_nxt, "rep", up)
    g_near = lax.ppermute(g_prv, "rep", down)
    pos = after(pos, g_nxt, u_nxt, g_prv, u_prv)
    g_sum = lax.ppermute(add(g_nxt, g_far), "rep", up)
    u_sum = lax.ppermute(add(u_prv, u_far), "rep", down)

    own_d = down_part(pos, 0, F32, 1)[0]
    own_g, own_u = gate_up_part(pos, 0, F32)

    x_mine, x_other = call(
        token_kernel,
        (steps,),
        [full(2 * count, total), out_col],
        [pl.BlockSpec((count, wcol), lambda i, p: (0, i))] * 2,
        [sds((count, half), BF)] * 2,
        (pos, sel_t, back),
    )
    x_got = lax.ppermute(x_other, "pair", swap)
    first = core == 0
    x_grad = jnp.concatenate(
        [jnp.where(first, x_mine, x_got), jnp.where(first, x_got, x_mine)], axis=1
    )

    gate_grad = own_g + g_sum.astype(F32) + g_near.astype(F32)
    up_grad = own_u + u_sum.astype(F32) + u_near.astype(F32)
    d_low = d_sum_u.astype(F32) + d_near_d.astype(F32)
    d_high = d_near_u.astype(F32) + d_sum_d.astype(F32)
    down_grad = own_d + jnp.concatenate([d_low, d_high], axis=0)
    return (x_grad, gate_grad[None], up_grad[None], down_grad[None])


def solution(mesh):
    rows = P(("pair", "wide", "rep"), None)
    in_specs = (rows, rows, rows, rows) + (
        P("wide", None, "pair"),
        P("wide", None, "pair"),
        P("wide", "pair", None),
    )
    out_specs = (
        rows,
        P("wide", "rep", "pair"),
        P("wide", "rep", "pair"),
        P("wide", "pair", "rep"),
    )
    return jax.shard_map(body, mesh=mesh, in_specs=in_specs, out_specs=out_specs, check_vma=False)
```

time: 352 us -> 228 us (0.65)
  waiting for transfers between devices: 176 us -> 72.1 us
  local copies, waits for them, and re-layouts: 61.8 us -> 8.18 us
  Pallas kernels: 0 us -> 40.5 us
  matrix products: 34.7 us -> 0 us
  starting transfers between devices: 16.5 us -> 41.8 us
  blocking collectives: 37.2 us -> 55.1 us
  between operations: 14 us -> 1.02 us
    unnamed x5 -> x0, waiting for transfers between devices: 129 us -> none
    ppermute x0 -> x20, waiting for transfers between devices: none -> 72.1 us  [the longest x1 49.3 us: body(): u_far = lax.ppermute(u_far, 'rep', down)]
    pallas_call x0 -> x15, Pallas kernels: none -> 40.5 us  [call(): pl.pallas_call(kernel, grid_spec=spec, out_shape=out_shape, compiler_para...]
    dot_general x11 -> x0, matrix products: 34.7 us -> none  [the longest x1 5.84 us: body(): jnp.einsum('secd,efd->secf', expert_grad, down_weight, preferred_element_...]
    all_to_all x2 -> x1, waiting for transfers between devices: 33.2 us -> 0.01 us  [body(): lax.all_to_all(row_grad.reshape(wide, 2 * CAP, half), 'wide', split_axis=...]
    ppermute x0 -> x20, starting transfers between devices: none -> 32.7 us  [the longest x1 4.01 us: body(): d_near_u = lax.ppermute(nxt[1], 'rep', up)]
    reshape x5 -> x0, local copies, waits for them, and re-layouts: 23.8 us -> none  [the longest x1 9.38 us: body(): partial_value = partial_value.reshape(pair_count, -1, features)]
    all_to_all x1, blocking collectives: 37.2 us -> 55.1 us  [body(): lax.all_to_all(sent, 'wide', split_axis=0, concat_axis=0, tiled=True)]
  transfers between devices with their start and end apart: 6 -> 21, of which waited for: 4 -> 8; matrix products, arithmetic and copies ran while one was open for 15% -> 3% of each run, Pallas kernels for 0% -> 13%
where the time goes in v1:
time: 228 us; the launch traced here: 227 us
  waiting for transfers between devices  72.1 us (32%)
  blocking collectives  55.1 us (24%)
  starting transfers between devices  41.8 us (18%)
  Pallas kernels  40.5 us (18%)
  other arithmetic  8.42 us (4%)
  local copies, waits for them, and re-layouts  8.18 us (4%)
    all_to_all x1, blocking collectives, body(): lax.all_to_all(sent, 'wide', split_axis=0, concat_axis=0, tiled=True)  55.1 us
    ppermute x1, waiting for transfers between devices, body(): u_far = lax.ppermute(u_far, 'rep', down)  49.3 us
    pallas_call x15, Pallas kernels, call(): pl.pallas_call(kernel, grid_spec=spec, out_shape=out_shape, compiler_para...  40.5 us
    all_to_all x1, starting transfers between devices, body(): lax.all_to_all(row_grad.reshape(wide, 2 * CAP, half), 'wide', split_axis=...  9.12 us
    unnamed x58, local copies, waits for them, and re-layouts  7.93 us
    ppermute x1, waiting for transfers between devices, body(): u_sum = lax.ppermute(add(u_prv, u_far), 'rep', down)  7.66 us
    ppermute x1, waiting for transfers between devices, body(): d_sum_u = lax.ppermute(add(nxt[0], d_far_u), 'rep', up)  6.36 us
    broadcast_in_dim x3, other arithmetic, body(): return (x_grad, gate_grad[None], up_grad[None], down_grad[None])  5.33 us
  transfers between devices with their start and end apart: 21, of which 8 were waited for; matrix products, arithmetic and copies ran while one was open for 3% of the time, Pallas kernels for 13%

profile of v1, /device:TPU:33, one launch (start us, length us, event | category | flops | bytes accessed | tf_op | source)
XLA Modules:
  0.0 227.2 jit_solution(10100887737204637298)
XLA Ops:
  0.6 0.8 collective-permute-start.2
  1.4 0.1 collective-permute-start.3
  1.5 0.4 collective-permute-start
  1.9 0.1 collective-permute-start.1
  2.0 0.6 pad_add_fusion.pos
  2.6 1.6 collective-permute-done.ids_b
  4.3 0.6 copy-done.27
  4.9 0.3 copy-done.19
  5.1 0.8 copy-done.20
  6.0 6.7 %shard_map.102 = (bf16[32,2,24,1280]{3,2,1,0:T(8,128)(2,1)}, bf16[256,768]{1,0:T(8,128)(2,1)}) custom-call(s32[2]{0:T(128)} %pad_add_fusion.pos, s32[6,128]{1,0:T(8,128)} %bitcast.41, s32[6,128]{1,0:T(8,128)} %copy-done.27, f32[6,128]{1,0:T(8,128)} %bitcast.43, f32[6,128]{1,0:T(8,128)} %copy-done.28, bf16[128,2560]{1,0:T(8,128)(2,1)} %tok_a.1, ...), custom_call_target="tpu_custom_call" | custom-call | flops 1 | bytes 1 | tf_op jit(solution)/shard_map/pallas_call | solution.py:28
  12.7 55.1 %all_to_all.10 = bf16[32,2,24,1280]{3,2,1,0:T(8,128)(2,1)S(1)} all-to-all(bf16[32,2,24,1280]{3,2,1,0:T(8,128)(2,1)} %get-tuple-element.47), channel_id=1, replica_groups=mesh['pair'=2,'wide'=32,'rep'=4] {'wide'}, dimensions={0} | all-to-all | bytes 7864320 | tf_op jit(solution)/shard_map/all_to_all | solution.py:217
  67.8 0.3 fusion.1
  68.0 1.7 collective-permute-start.4
  69.8 0.1 collective-permute-start.5
  69.9 0.6 copy-done.9
  70.5 2.8 %shard_map.103 = (bf16[2560,384]{1,0:T(8,128)(2,1)S(1)}, bf16[2560,768]{1,0:T(8,128)(2,1)S(1)}, bf16[768,2560]{1,0:T(8,128)(2,1)S(1)}) custom-call(s32[2]{0:T(128)S(1)} %copy-done.15, bf16[384,2560]{1,0:T(8,128)(2,1)S(1)} %bitcast.37, bf16[2560,384]{1,0:T(8,128)(2,1)S(1)} %bitcast.38, bf16[2560,384]{1,0:T(8,128)(2,1)S(1)} %bitcast.39), custom_call_target="tpu_custom_call" | custom-call | flops 1 | bytes 1 | tf_op jit(solution)/shard_map/pallas_call | solution.py:28
  73.4 4.8 %shard_map.104 = (bf16[2,1280,768]{2,1,0:T(8,128)(2,1)S(1)}, bf16[384,768]{1,0:T(8,128)(2,1)S(1)}, f32[768,768]{1,0:T(8,128)S(1)}) custom-call(s32[2]{0:T(128)S(1)} %copy-done.15, bf16[768,1280]{1,0:T(8,128)(2,1)S(1)} %bitcast.36, bf16[768,1280]{1,0:T(8,128)(2,1)S(1)} %collective-permute-done.4.x_b, bf16[2,1280,768]{2,1,0:T(8,128)(2,1)S(1)} %bitcast.30, ...), custom_call_target="tpu_custom_call" | custom-call | flops 1 | bytes 1 | tf_op jit(solution)/shard_map/pallas_call | solution.py:28
  78.2 1.3 shard_map.105
  79.6 3.1 %collective-permute-start.6 = (bf16[192,640]{1,0:T(8,128)(2,1)S(1)}, bf16[192,640]{1,0:T(8,128)(2,1)S(1)}, u32[]{:S(2)}, u32[]{:S(2)}) collective-permute-start(bf16[192,640]{1,0:T(8,128)(2,1)S(1)} %get-tuple-element.54), channel_id=1, source_target_pairs={{0,1},{1,2},{2,3},{3,0},{4,5},{5,6},{6,7},{7,4},{8,9},{9,10},{10,1... | collective-permute-start | bytes 737288 | tf_op jit(solution)/shard_map/ppermute | solution.py:279
  82.6 2.2 collective-permute-start.7
  84.9 1.3 shard_map.107
  86.2 1.5 shard_map.106
  87.8 3.1 %shard_map.108.backs = bf16[768,768]{1,0:T(8,128)(2,1)S(1)} custom-call(s32[2]{0:T(128)S(1)} %copy-done.15, bf16[768,1280]{1,0:T(8,128)(2,1)S(1)} %bitcast.24, bf16[768,1280]{1,0:T(8,128)(2,1)S(1)} %collective-permute-done.5.g_b, bf16[2,1280,384]{2,1,0:T(8,128)(2,1)S(1)} %bitcast.33, bf16[2,1280,384]{2,1,0:T(8,128)(2,1)S(1)} %bitcast.34, ...), custom_call_target="tpu_custom_call" | custom-call | flops 1 | bytes 1 | tf_op jit(solution)/shard_map/pallas_call | solution.py:28
  90.9 2.9 %collective-permute-done.6 = bf16[192,640]{1,0:T(8,128)(2,1)S(1)} collective-permute-done((bf16[192,640]{1,0:T(8,128)(2,1)S(1)}, bf16[192,640]{1,0:T(8,128)(2,1)S(1)}, u32[]{:S(2)}, u32[]{:S(2)}) %collective-permute-start.6) | collective-permute-done | bytes 245792 | tf_op jit(solution)/shard_map/ppermute | solution.py:279
  93.8 2.8 %shard_map.109 = bf16[768,1280]{1,0:T(8,128)(2,1)S(1)} custom-call(s32[2]{0:T(128)S(1)} %copy-done.15, bf16[768,768]{1,0:T(8,128)(2,1)S(1)} %shard_map.108.backs, bf16[768,2560]{1,0:T(8,128)(2,1)S(1)} %get-tuple-element.64.wgu), custom_call_target="tpu_custom_call" | custom-call | flops 1 | bytes 1 | tf_op jit(solution)/shard_map/pallas_call | solution.py:28
  96.6 2.7 %collective-permute-start.8 = (bf16[768,1280]{1,0:T(8,128)(2,1)S(1)}, bf16[768,1280]{1,0:T(8,128)(2,1)S(1)}, u32[]{:S(2)}, u32[]{:S(2)}) collective-permute-start(bf16[768,1280]{1,0:T(8,128)(2,1)S(1)} %shard_map.109), channel_id=1, source_target_pairs={{0,128},{128,0},{1,129},{129,1},{2,130},{130,2},{3,131},{131,3},{4... | collective-permute-start | bytes 5898248 | tf_op jit(solution)/shard_map/ppermute | solution.py:310
  99.3 1.3 collective-permute-start.10
  100.6 4.0 %collective-permute-start.9 = (bf16[192,640]{1,0:T(8,128)(2,1)S(1)}, bf16[192,640]{1,0:T(8,128)(2,1)S(1)}, u32[]{:S(2)}, u32[]{:S(2)}) collective-permute-start(bf16[192,640]{1,0:T(8,128)(2,1)S(1)} %get-tuple-element.58), channel_id=1, source_target_pairs={{0,1},{1,2},{2,3},{3,0},{4,5},{5,6},{6,7},{7,4},{8,9},{9,10},{10,1... | collective-permute-start | bytes 737288 | tf_op jit(solution)/shard_map/ppermute | solution.py:284
  104.7 0.1 collective-permute-start.12
  104.8 0.1 add_convert_fusion.3
  104.8 3.7 %collective-permute-start.11 = (bf16[192,640]{1,0:T(8,128)(2,1)S(1)}, bf16[192,640]{1,0:T(8,128)(2,1)S(1)}, u32[]{:S(2)}, u32[]{:S(2)}) collective-permute-start(bf16[192,640]{1,0:T(8,128)(2,1)S(1)} %add_convert_fusion.3), channel_id=1, source_target_pairs={{0,1},{1,2},{2,3},{3,0},{4,5},{5,6},{6,7},{7,4},{8,9},{9,10},{10,1... | collective-permute-start | bytes 737288 | tf_op jit(solution)/shard_map/ppermute | solution.py:297
  108.5 1.5 shard_map.110
  110.0 2.8 %shard_map.111 = bf16[768,1280]{1,0:T(8,128)(2,1)S(1)} custom-call(s32[2]{0:T(128)S(1)} %copy-done.15, bf16[768,768]{1,0:T(8,128)(2,1)S(1)} %shard_map.108.backs, bf16[768,2560]{1,0:T(8,128)(2,1)S(1)} %get-tuple-element.64.wgu, bf16[768,1280]{1,0:T(8,128)(2,1)S(1)} %collective-permute-done.8.got), custom_call_target="tpu_custom_call" | custom-call | flops 1 | bytes 1 | tf_op jit(solution)/shard_map/pallas_call | solution.py:28
  112.8 1.3 copy-done.6
  114.2 0.7 copy-done.21
  114.9 2.1 collective-permute-done.12
  117.0 0.7 copy-done.23
  117.7 6.4 %collective-permute-done.11 = bf16[192,640]{1,0:T(8,128)(2,1)S(1)} collective-permute-done((bf16[192,640]{1,0:T(8,128)(2,1)S(1)}, bf16[192,640]{1,0:T(8,128)(2,1)S(1)}, u32[]{:S(2)}, u32[]{:S(2)}) %collective-permute-start.11) | collective-permute-done | bytes 245792 | tf_op jit(solution)/shard_map/ppermute | solution.py:297
  124.0 0.7 copy-done.25
  124.7 9.1 %all-to-all-start.1 = ((bf16[32,24,1280]{2,1,0:T(8,128)(2,1)}), bf16[32,24,1280]{2,1,0:T(8,128)(2,1)}, u32[]{:S(2)}, u32[]{:S(2)}) async-start(bf16[32,24,1280]{2,1,0:T(8,128)(2,1)} %bitcast.32), calls=%async_computation.1 | async-start | bytes 3932160 | tf_op jit(solution)/shard_map/all_to_all | solution.py:325
  133.8 1.6 collective-permute-start.17
  135.4 2.1 copy-done.1
  137.5 2.3 %shard_map.113 = (bf16[640,384]{1,0:T(8,128)(2,1)}, bf16[640,384]{1,0:T(8,128)(2,1)S(1)}) custom-call(s32[2]{0:T(128)S(1)} %copy-done.15, bf16[2560,768]{1,0:T(8,128)(2,1)S(1)} %bitcast.27, bf16[768,768]{1,0:T(8,128)(2,1)S(1)} %shard_map.108.backs), custom_call_target="tpu_custom_call" | custom-call | flops 1 | bytes 1 | tf_op jit(solution)/shard_map/pallas_call | solution.py:28
  139.8 2.3 shard_map.112
  142.1 0.9 collective-permute-start.19
  142.9 2.7 %collective-permute-start.16 = (bf16[640,384]{1,0:T(8,128)(2,1)}, bf16[640,384]{1,0:T(8,128)(2,1)}, u32[]{:S(2)}, u32[]{:S(2)}) collective-permute-start(bf16[640,384]{1,0:T(8,128)(2,1)} %get-tuple-element.75), channel_id=1, source_target_pairs={{0,3},{1,0},{2,1},{3,2},{4,7},{5,4},{6,5},{7,6},{8,11},{9,8},{10,9... | collective-permute-start | bytes 1474568 | tf_op jit(solution)/shard_map/ppermute | solution.py:333
  145.6 1.5 shard_map.115
  147.2 0.9 collective-permute-start.14
  148.0 1.3 shard_map.116
  149.4 0.1 convert_add_fusion
  149.6 49.3 %collective-permute-done.17 = bf16[640,384]{1,0:T(8,128)(2,1)} collective-permute-done((bf16[640,384]{1,0:T(8,128)(2,1)}, bf16[640,384]{1,0:T(8,128)(2,1)}, u32[]{:S(2)}, u32[]{:S(2)}) %collective-permute-start.17) | collective-permute-done | bytes 491552 | tf_op jit(solution)/shard_map/ppermute | solution.py:329
  198.8 1.2 add_convert_fusion
  200.0 2.0 collective-permute-start.18
  202.0 0.1 add_convert_fusion.1
  202.2 0.9 collective-permute-start.15
  203.1 1.0 fusion
  204.1 4.4 %shard_map.114 = (bf16[128,1280]{1,0:T(8,128)(2,1)S(1)}, bf16[128,1280]{1,0:T(8,128)(2,1)S(1)}) custom-call(s32[2]{0:T(128)S(1)} %copy-done.15, bf16[256,768]{1,0:T(8,128)(2,1)S(1)} %copy-done.14, bf16[768,1280]{1,0:T(8,128)(2,1)} %bitcast.13.rows), custom_call_target="tpu_custom_call" | custom-call | flops 1 | bytes 1 | tf_op jit(solution)/shard_map/pallas_call | solution.py:28
  208.5 3.6 %collective-permute-start.13 = (bf16[128,1280]{1,0:T(8,128)(2,1)S(1)}, bf16[128,1280]{1,0:T(8,128)(2,1)S(1)}, u32[]{:S(2)}, u32[]{:S(2)}) collective-permute-start(bf16[128,1280]{1,0:T(8,128)(2,1)S(1)} %get-tuple-element.81), channel_id=1, source_target_pairs={{0,128},{128,0},{1,129},{129,1},{2,130},{130,2},{3,131},{131,3},{4... | collective-permute-start | bytes 983048 | tf_op jit(solution)/shard_map/ppermute | solution.py:349
  212.1 7.7 %collective-permute-done.18 = bf16[640,384]{1,0:T(8,128)(2,1)S(1)} collective-permute-done((bf16[640,384]{1,0:T(8,128)(2,1)S(1)}, bf16[640,384]{1,0:T(8,128)(2,1)S(1)}, u32[]{:S(2)}, u32[]{:S(2)}) %collective-permute-start.18) | collective-permute-done | bytes 491552 | tf_op jit(solution)/shard_map/ppermute | solution.py:336
  219.8 2.1 add_bitcast_fusion
  221.9 2.1 collective-permute-done.15
  224.1 2.1 add_bitcast_fusion.1
  226.2 0.1 broadcast_select_fusion.1
  226.3 0.9 pad_maximum_fusion
  (64 shorter events, 0.3 us)
Async XLA Ops:
  0.6 3.7 %collective-permute-start.2 = (bf16[128,2560]{1,0:T(8,128)(2,1)}, bf16[128,2560]{1,0:T(8,128)(2,1)S(1)}, u32[]{:S(2)}, u32[]{:S(2)}) collective-permute-start(bf16[128,2560]{1,0:T(8,128)(2,1)} %tok_a.1), channel_id=1, source_target_pairs={{0,128},{128,0},{1,129},{129,1},{2,130},{130,2},{3,131},{131,3},{4... | collective-permute-start | bytes 1966088 | tf_op jit(solution)/shard_map/ppermute | solution.py:175
  1.4 2.9 %collective-permute-start.3 = (bf16[128,2560]{1,0:T(8,128)(2,1)}, bf16[128,2560]{1,0:T(8,128)(2,1)S(1)}, u32[]{:S(2)}, u32[]{:S(2)}) collective-permute-start(bf16[128,2560]{1,0:T(8,128)(2,1)} %og_a.1), channel_id=1, source_target_pairs={{0,128},{128,0},{1,129},{129,1},{2,130},{130,2},{3,131},{131,3},{4... | collective-permute-start | bytes 1966088 | tf_op jit(solution)/shard_map/ppermute | solution.py:176
  1.5 2.8 %collective-permute-start = (s32[6,128]{1,0:T(8,128)}, s32[6,128]{1,0:T(8,128)S(1)}, u32[]{:S(2)}, u32[]{:S(2)}) collective-permute-start(s32[6,128]{1,0:T(8,128)} %bitcast.40), channel_id=1, source_target_pairs={{0,128},{128,0},{1,129},{129,1},{2,130},{130,2},{3,131},{131,3},{4... | collective-permute-start | bytes 9224 | tf_op jit(solution)/shard_map/ppermute | solution.py:173
  1.9 2.4 %collective-permute-start.1 = (f32[6,128]{1,0:T(8,128)}, f32[6,128]{1,0:T(8,128)S(1)}, u32[]{:S(2)}, u32[]{:S(2)}) collective-permute-start(f32[6,128]{1,0:T(8,128)} %bitcast.42), channel_id=1, source_target_pairs={{0,128},{128,0},{1,129},{129,1},{2,130},{130,2},{3,131},{131,3},{4... | collective-permute-start | bytes 9224 | tf_op jit(solution)/shard_map/ppermute | solution.py:174
  4.3 0.6 copy-start.27
  4.3 0.6 copy-start.28
  4.3 0.8 copy-start.19
  5.1 0.8 copy-start.20
  67.8 2.1 copy-start.7
  67.8 2.1 copy-start.8
  67.8 2.7 %copy-start.9 = (bf16[1,2560,384]{2,1,0:T(8,128)(2,1)S(1)}, bf16[1,2560,384]{2,1,0:T(8,128)(2,1)}, u32[]{:S(2)}) copy-start(bf16[1,2560,384]{2,1,0:T(8,128)(2,1)} %param.12) | copy-start | bytes 5898244
  67.8 2.7 %copy-start.15 = (s32[2]{0:T(128)S(1)}, s32[2]{0:T(128)}, u32[]{:S(2)}) copy-start(s32[2]{0:T(128)} %pad_add_fusion.pos) | copy-start | bytes 28
  68.0 5.3 %collective-permute-start.4 = (bf16[768,1280]{1,0:T(8,128)(2,1)S(1)}, bf16[768,1280]{1,0:T(8,128)(2,1)S(1)}, u32[]{:S(2)}, u32[]{:S(2)}) collective-permute-start(bf16[768,1280]{1,0:T(8,128)(2,1)S(1)} %bitcast.35), channel_id=1, source_target_pairs={{0,128},{128,0},{1,129},{129,1},{2,130},{130,2},{3,131},{131,3},{4... | collective-permute-start | bytes 5898248 | tf_op jit(solution)/shard_map/ppermute | solution.py:220
  69.8 8.5 %collective-permute-start.5 = (bf16[768,1280]{1,0:T(8,128)(2,1)S(1)}, bf16[768,1280]{1,0:T(8,128)(2,1)S(1)}, u32[]{:S(2)}, u32[]{:S(2)}) collective-permute-start(bf16[768,1280]{1,0:T(8,128)(2,1)S(1)} %bitcast.20), channel_id=1, source_target_pairs={{0,128},{128,0},{1,129},{129,1},{2,130},{130,2},{3,131},{131,3},{4... | collective-permute-start | bytes 5898248 | tf_op jit(solution)/shard_map/ppermute | solution.py:249
  78.2 8.0 %copy-start.4 = (bf16[384,768]{1,0:T(8,128)(2,1)}, bf16[384,768]{1,0:T(8,128)(2,1)S(1)}, u32[]{:S(2)}) copy-start(bf16[384,768]{1,0:T(8,128)(2,1)S(1)} %get-tuple-element.52.hidden_t) | copy-start | bytes 1769476
  78.2 30.3 %copy-start = (bf16[2,1280,768]{2,1,0:T(8,128)(2,1)}, bf16[2,1280,768]{2,1,0:T(8,128)(2,1)S(1)}, u32[]{:S(2)}) copy-start(bf16[2,1280,768]{2,1,0:T(8,128)(2,1)S(1)} %get-tuple-element.66) | copy-start | bytes 11796484
  78.2 9.6 %copy-start.2 = (bf16[768,1280]{1,0:T(8,128)(2,1)}, bf16[768,1280]{1,0:T(8,128)(2,1)S(1)}, u32[]{:S(2)}) copy-start(bf16[768,1280]{1,0:T(8,128)(2,1)S(1)} %collective-permute-done.5.g_b) | copy-start | bytes 5898244
  79.6 14.2 %collective-permute-start.6 = (bf16[192,640]{1,0:T(8,128)(2,1)S(1)}, bf16[192,640]{1,0:T(8,128)(2,1)S(1)}, u32[]{:S(2)}, u32[]{:S(2)}) collective-permute-start(bf16[192,640]{1,0:T(8,128)(2,1)S(1)} %get-tuple-element.54), channel_id=1, source_target_pairs={{0,1},{1,2},{2,3},{3,0},{4,5},{5,6},{6,7},{7,4},{8,9},{9,10},{10,1... | collective-permute-start | bytes 737288 | tf_op jit(solution)/shard_map/ppermute | solution.py:279
  82.6 11.2 %collective-permute-start.7 = (bf16[192,640]{1,0:T(8,128)(2,1)S(1)}, bf16[192,640]{1,0:T(8,128)(2,1)S(1)}, u32[]{:S(2)}, u32[]{:S(2)}) collective-permute-start(bf16[192,640]{1,0:T(8,128)(2,1)S(1)} %get-tuple-element.55), channel_id=1, source_target_pairs={{0,3},{1,0},{2,1},{3,2},{4,7},{5,4},{6,5},{7,6},{8,11},{9,8},{10,9... | collective-permute-start | bytes 737288 | tf_op jit(solution)/shard_map/ppermute | solution.py:280
  96.6 13.4 %collective-permute-start.8 = (bf16[768,1280]{1,0:T(8,128)(2,1)S(1)}, bf16[768,1280]{1,0:T(8,128)(2,1)S(1)}, u32[]{:S(2)}, u32[]{:S(2)}) collective-permute-start(bf16[768,1280]{1,0:T(8,128)(2,1)S(1)} %shard_map.109), channel_id=1, source_target_pairs={{0,128},{128,0},{1,129},{129,1},{2,130},{130,2},{3,131},{131,3},{4... | collective-permute-start | bytes 5898248 | tf_op jit(solution)/shard_map/ppermute | solution.py:310
  99.3 14.9 %collective-permute-start.10 = (bf16[192,640]{1,0:T(8,128)(2,1)S(1)}, bf16[192,640]{1,0:T(8,128)(2,1)S(1)}, u32[]{:S(2)}, u32[]{:S(2)}) collective-permute-start(bf16[192,640]{1,0:T(8,128)(2,1)S(1)} %get-tuple-element.59), channel_id=1, source_target_pairs={{0,3},{1,0},{2,1},{3,2},{4,7},{5,4},{6,5},{7,6},{8,11},{9,8},{10,9... | collective-permute-start | bytes 737288 | tf_op jit(solution)/shard_map/ppermute | solution.py:285
  100.6 13.6 %collective-permute-start.9 = (bf16[192,640]{1,0:T(8,128)(2,1)S(1)}, bf16[192,640]{1,0:T(8,128)(2,1)S(1)}, u32[]{:S(2)}, u32[]{:S(2)}) collective-permute-start(bf16[192,640]{1,0:T(8,128)(2,1)S(1)} %get-tuple-element.58), channel_id=1, source_target_pairs={{0,1},{1,2},{2,3},{3,0},{4,5},{5,6},{6,7},{7,4},{8,9},{9,10},{10,1... | collective-permute-start | bytes 737288 | tf_op jit(solution)/shard_map/ppermute | solution.py:284
  104.7 12.3 %collective-permute-start.12 = (bf16[192,640]{1,0:T(8,128)(2,1)S(1)}, bf16[192,640]{1,0:T(8,128)(2,1)S(1)}, u32[]{:S(2)}, u32[]{:S(2)}) collective-permute-start(bf16[192,640]{1,0:T(8,128)(2,1)S(1)} %add_convert_fusion.2), channel_id=1, source_target_pairs={{0,3},{1,0},{2,1},{3,2},{4,7},{5,4},{6,5},{7,6},{8,11},{9,8},{10,9... | collective-permute-start | bytes 737288 | tf_op jit(solution)/shard_map/ppermute | solution.py:298
  104.8 19.2 %collective-permute-start.11 = (bf16[192,640]{1,0:T(8,128)(2,1)S(1)}, bf16[192,640]{1,0:T(8,128)(2,1)S(1)}, u32[]{:S(2)}, u32[]{:S(2)}) collective-permute-start(bf16[192,640]{1,0:T(8,128)(2,1)S(1)} %add_convert_fusion.3), channel_id=1, source_target_pairs={{0,1},{1,2},{2,3},{3,0},{4,5},{5,6},{6,7},{7,4},{8,9},{9,10},{10,1... | collective-permute-start | bytes 737288 | tf_op jit(solution)/shard_map/ppermute | solution.py:297
  110.0 2.8 %copy-start.16 = (bf16[640,384]{1,0:T(8,128)(2,1)}, bf16[640,384]{1,0:T(8,128)(2,1)S(1)}, u32[]{:S(2)}) copy-start(bf16[640,384]{1,0:T(8,128)(2,1)S(1)} %get-tuple-element.83) | copy-start | bytes 1474564
  110.0 2.8 %copy-start.18 = (bf16[640,384]{1,0:T(8,128)(2,1)}, bf16[640,384]{1,0:T(8,128)(2,1)S(1)}, u32[]{:S(2)}) copy-start(bf16[640,384]{1,0:T(8,128)(2,1)S(1)} %get-tuple-element.85) | copy-start | bytes 1474564
  112.8 1.3 copy-start.6
  114.2 0.7 copy-start.21
  117.0 0.7 copy-start.23
  124.0 0.7 copy-start.25
  124.7 79.4 %all-to-all-start.1 = ((bf16[32,24,1280]{2,1,0:T(8,128)(2,1)}), bf16[32,24,1280]{2,1,0:T(8,128)(2,1)}, u32[]{:S(2)}, u32[]{:S(2)}) async-start(bf16[32,24,1280]{2,1,0:T(8,128)(2,1)} %bitcast.32), calls=%async_computation.1 | async-start | bytes 3932160 | tf_op jit(solution)/shard_map/all_to_all | solution.py:325
  133.8 65.0 %collective-permute-start.17 = (bf16[640,384]{1,0:T(8,128)(2,1)}, bf16[640,384]{1,0:T(8,128)(2,1)}, u32[]{:S(2)}, u32[]{:S(2)}) collective-permute-start(bf16[640,384]{1,0:T(8,128)(2,1)} %copy-done.18), channel_id=1, source_target_pairs={{0,3},{1,0},{2,1},{3,2},{4,7},{5,4},{6,5},{7,6},{8,11},{9,8},{10,9... | collective-permute-start | bytes 1474568 | tf_op jit(solution)/shard_map/ppermute | solution.py:329
  135.4 2.1 copy-start.1
  142.1 70.1 %collective-permute-start.19 = (bf16[640,384]{1,0:T(8,128)(2,1)}, bf16[640,384]{1,0:T(8,128)(2,1)}, u32[]{:S(2)}, u32[]{:S(2)}) collective-permute-start(bf16[640,384]{1,0:T(8,128)(2,1)} %get-tuple-element.74), channel_id=1, source_target_pairs={{0,1},{1,2},{2,3},{3,0},{4,5},{5,6},{6,7},{7,4},{8,9},{9,10},{10,1... | collective-permute-start | bytes 1474568 | tf_op jit(solution)/shard_map/ppermute | solution.py:332
  142.9 79.0 %collective-permute-start.16 = (bf16[640,384]{1,0:T(8,128)(2,1)}, bf16[640,384]{1,0:T(8,128)(2,1)}, u32[]{:S(2)}, u32[]{:S(2)}) collective-permute-start(bf16[640,384]{1,0:T(8,128)(2,1)} %get-tuple-element.75), channel_id=1, source_target_pairs={{0,3},{1,0},{2,1},{3,2},{4,7},{5,4},{6,5},{7,6},{8,11},{9,8},{10,9... | collective-permute-start | bytes 1474568 | tf_op jit(solution)/shard_map/ppermute | solution.py:333
  145.6 1.5 copy-start.17
  145.6 2.4 %copy-start.3 = (bf16[768,1280]{1,0:T(8,128)(2,1)S(1)}, bf16[768,1280]{1,0:T(8,128)(2,1)}, u32[]{:S(2)}) copy-start(bf16[768,1280]{1,0:T(8,128)(2,1)} %copy-done.2) | copy-start | bytes 5898244
  145.6 2.4 %copy-start.5 = (bf16[384,768]{1,0:T(8,128)(2,1)S(1)}, bf16[384,768]{1,0:T(8,128)(2,1)}, u32[]{:S(2)}) copy-start(bf16[384,768]{1,0:T(8,128)(2,1)} %copy-done.4) | copy-start | bytes 1769476
  147.1 2.3 copy-start.10
  147.1 2.3 copy-start.12
  147.2 2.3 copy-start.22
  147.2 2.3 copy-start.24
  147.2 2.3 copy-start.26
  147.2 54.8 %collective-permute-start.14 = (bf16[640,384]{1,0:T(8,128)(2,1)S(1)}, bf16[640,384]{1,0:T(8,128)(2,1)S(1)}, u32[]{:S(2)}, u32[]{:S(2)}) collective-permute-start(bf16[640,384]{1,0:T(8,128)(2,1)S(1)} %copy-done.17), channel_id=1, source_target_pairs={{0,1},{1,2},{2,3},{3,0},{4,5},{5,6},{6,7},{7,4},{8,9},{9,10},{10,1... | collective-permute-start | bytes 1474568 | tf_op jit(solution)/shard_map/ppermute | solution.py:328
  200.0 4.1 %copy-start.14 = (bf16[256,768]{1,0:T(8,128)(2,1)S(1)}, bf16[256,768]{1,0:T(8,128)(2,1)}, u32[]{:S(2)}) copy-start(bf16[256,768]{1,0:T(8,128)(2,1)} %get-tuple-element.78.sel) | copy-start | bytes 1179652
  200.0 19.8 %collective-permute-start.18 = (bf16[640,384]{1,0:T(8,128)(2,1)S(1)}, bf16[640,384]{1,0:T(8,128)(2,1)S(1)}, u32[]{:S(2)}, u32[]{:S(2)}) collective-permute-start(bf16[640,384]{1,0:T(8,128)(2,1)S(1)} %add_convert_fusion), channel_id=1, source_target_pairs={{0,3},{1,0},{2,1},{3,2},{4,7},{5,4},{6,5},{7,6},{8,11},{9,8},{10,9... | collective-permute-start | bytes 1474568 | tf_op jit(solution)/shard_map/ppermute | solution.py:336
  202.2 21.9 %collective-permute-start.15 = (bf16[640,384]{1,0:T(8,128)(2,1)S(1)}, bf16[640,384]{1,0:T(8,128)(2,1)S(1)}, u32[]{:S(2)}, u32[]{:S(2)}) collective-permute-start(bf16[640,384]{1,0:T(8,128)(2,1)S(1)} %add_convert_fusion.1), channel_id=1, source_target_pairs={{0,1},{1,2},{2,3},{3,0},{4,5},{5,6},{6,7},{7,4},{8,9},{9,10},{10,1... | collective-permute-start | bytes 1474568 | tf_op jit(solution)/shard_map/ppermute | solution.py:335
  203.1 16.7 %copy-start.13 = (f32[640,384]{1,0:T(8,128)S(1)}, f32[640,384]{1,0:T(8,128)}, u32[]{:S(2)}) copy-start(f32[640,384]{1,0:T(8,128)} %copy-done.12) | copy-start | bytes 2949124
  208.5 15.5 %copy-start.11 = (f32[640,384]{1,0:T(8,128)S(1)}, f32[640,384]{1,0:T(8,128)}, u32[]{:S(2)}) copy-start(f32[640,384]{1,0:T(8,128)} %copy-done.10) | copy-start | bytes 2949124
  208.5 17.7 %collective-permute-start.13 = (bf16[128,1280]{1,0:T(8,128)(2,1)S(1)}, bf16[128,1280]{1,0:T(8,128)(2,1)S(1)}, u32[]{:S(2)}, u32[]{:S(2)}) collective-permute-start(bf16[128,1280]{1,0:T(8,128)(2,1)S(1)} %get-tuple-element.81), channel_id=1, source_target_pairs={{0,128},{128,0},{1,129},{129,1},{2,130},{130,2},{3,131},{131,3},{4... | collective-permute-start | bytes 983048 | tf_op jit(solution)/shard_map/ppermute | solution.py:349

commit v2 on v1

--- a/solution.py
+++ b/solution.py
@@ -4,7 +4,7 @@
 from jax import lax
 from jax.experimental import pallas as pl
 from jax.experimental.pallas import tpu as pltpu
-from jax.sharding import PartitionSpec as P
+from jax.sharding import Mesh, PartitionSpec as P
 
 WINDOW = 32
 CAP = 12
@@ -17,7 +17,7 @@
     return lax.dot_general(a, b, (((ca,), (cb,)), ((), ())), preferred_element_type=F32)
 
 
-def call(kernel, grid, in_specs, out_specs, out_shape, args, scratch=(), grant=24):
+def call(kernel, grid, in_specs, out_specs, out_shape, args, scratch=(), grant=24, cost=1):
     spec = pltpu.PrefetchScalarGridSpec(
         num_scalar_prefetch=1,
         grid=grid,
@@ -32,7 +32,7 @@
         compiler_params=pltpu.CompilerParams(
             dimension_semantics=("arbitrary",) * len(grid), vmem_limit_bytes=grant * MIB
         ),
-        cost_estimate=pl.CostEstimate(flops=1, bytes_accessed=1, transcendentals=0),
+        cost_estimate=pl.CostEstimate(flops=1, bytes_accessed=cost, transcendentals=0),
     )(*args)
 
 
@@ -54,7 +54,7 @@
     return code, gate
 
 
-def pack_kernel(pos, ids_a, ids_b, gv_a, gv_b, tok_a, tok_b, og_a, og_b, out, sel_t, sel, scale):
+def pack_kernel(pos, ids_a, ids_b, gv_a, gv_b, tok_a, tok_b, og_a, og_b, out, keep, give, sel, scale):
     @pl.when(pl.program_id(0) == 0)
     def _():
         core = pos[0]
@@ -65,10 +65,14 @@
         width = code.shape[1]
         slot = lax.broadcasted_iota(jnp.int32, (WINDOW, 2 * CAP, width), 1)
         hit = code[:, None, :] == slot
-        picked = jnp.where(hit, 1.0, 0.0).reshape(WINDOW * 2 * CAP, width).astype(BF)
+        picked = jnp.where(hit, 1.0, 0.0)
         weight = jnp.where(hit, gate[:, None, :], 0.0).reshape(WINDOW * 2 * CAP, width)
-        sel[...] = picked
-        sel_t[...] = picked.T
+        sel[...] = picked.reshape(WINDOW * 2 * CAP, width).astype(BF)
+        split = picked.reshape(WINDOW // 2, 2, 2 * CAP, width)
+        even = split[:, 0].reshape(WINDOW * CAP, width).astype(BF).T
+        odd = split[:, 1].reshape(WINDOW * CAP, width).astype(BF).T
+        keep[...] = jnp.where(pos[2] == 0, even, odd)
+        give[...] = jnp.where(pos[2] == 0, odd, even)
         scale[...] = jnp.sum(weight, axis=1, keepdims=True)
 
     shape = (WINDOW, 2 * CAP, out.shape[3])
@@ -142,11 +146,11 @@
     out[...] = (value + got[...].astype(F32)).astype(out.dtype)
 
 
-def token_kernel(pos, sel, rows, own, other):
-    value = dot(sel[...], rows[...], 1, 0)
-    half = value.shape[0] // 2
-    own[...] = value[:half].astype(BF)
-    other[...] = value[half:].astype(BF)
+def token_kernel(pos, keep, got, rows_keep, rows_got, own, other):
+    for sel, rows, out in ((keep, rows_keep, own), (got, rows_got, other)):
+        n, _, slots, m = rows.shape
+        flat = rows[:, 0].astype(F32).reshape(n * slots, m).astype(BF)
+        out[...] = dot(sel[...], flat, 1, 0).astype(BF)
 
 
 def body(tokens, out_grad, expert_ids, gate_vals, gate_weight, up_weight, down_weight):
@@ -154,12 +158,15 @@
     half = features // 2
     quarter = features // 4
     hid = gate_weight.shape[2]
-    wide = lax.axis_size("wide")
+    plane = ("y", "x")
+    experts = ("y", "x", "zlo")
+    wide = lax.axis_size(experts)
     choices = expert_ids.shape[1]
     total = WINDOW * 2 * CAP
     core = lax.axis_index("pair").astype(jnp.int32)
     rep = lax.axis_index("rep").astype(jnp.int32)
-    pos = jnp.stack([core, rep])
+    parity = lax.axis_index("zlo").astype(jnp.int32)
+    pos = jnp.stack([core, rep, parity])
     swap = [(0, 1), (1, 0)]
     up = [(i, (i + 1) % 4) for i in range(4)]
     down = [(i, (i + 3) % 4) for i in range(4)]
@@ -182,15 +189,16 @@
     wcol = half // steps
     tok_spec = pl.BlockSpec((count, wcol), lambda i, p: (0, p[0] * steps + i))
     out_col = pl.BlockSpec((total, wcol), lambda i, p: (0, i))
-    sent, sel_t = call(
+    sent, keep, give = call(
         pack_kernel,
         (steps,),
         [full(choices, count)] * 4 + [tok_spec] * 4,
         [
             pl.BlockSpec((wide, 2, 2 * CAP, wcol), lambda i, p: (0, 0, 0, i)),
-            full(2 * count, total),
+            full(2 * count, total // 2),
+            full(2 * count, total // 2),
         ],
-        [sds((wide, 2, 2 * CAP, half), BF), sds((2 * count, total), BF)],
+        [sds((wide, 2, 2 * CAP, half), BF)] + [sds((2 * count, total // 2), BF)] * 2,
         (pos, ids, ids_b, gates, gv_b, tokens, tok_b, out_grad, og_b),
         scratch=[pltpu.VMEM((total, 2 * count), BF), pltpu.VMEM((total, 1), F32)],
         grant=56,
@@ -214,9 +222,10 @@
         (pos, wd, wg_full, wu_full),
     )
     pos = after(pos, wd_t)
-    landed = lax.all_to_all(sent, "wide", split_axis=0, concat_axis=0, tiled=True)
+    landed = lax.all_to_all(sent, experts, split_axis=0, concat_axis=0, tiled=True)
     x_own = landed[:, 0].reshape(total, half)
     g_own = landed[:, 1].reshape(total, half)
+    got = lax.ppermute(give, "zlo", swap)
     x_oth = lax.ppermute(x_own, "pair", swap)
 
     parts = 3
@@ -245,7 +254,7 @@
         (pos, x_own, x_oth, wgu, wgu),
     )
     x_t = x_t.reshape(features, total)
-    pos = after(pos, hidden_t)
+    pos = after(pos, hidden_t, got)
     g_oth = lax.ppermute(g_own, "pair", swap)
 
     def down_part(place, shift, dtype, pieces):
@@ -322,9 +331,10 @@
     row_grad, pos, g_far, u_far, d_near_u, d_near_d, d_sum_u, d_sum_d = lax.optimization_barrier(
         (row_grad, pos, g_far, u_far, d_near_u, d_near_d, d_sum_u, d_sum_d)
     )
+    nodes = wide // 2
     back = lax.all_to_all(
-        row_grad.reshape(wide, 2 * CAP, half), "wide", split_axis=0, concat_axis=0, tiled=True
-    ).reshape(total, half)
+        row_grad.reshape(nodes, 4 * CAP, half), plane, split_axis=0, concat_axis=0, tiled=True
+    ).reshape(nodes, 2, 2 * CAP, half)
     g_far = lax.ppermute(g_far, "rep", up)
     u_far = lax.ppermute(u_far, "rep", down)
     g_nxt, u_nxt = gate_up_part(pos, 1, BF)
@@ -332,20 +342,29 @@
     u_near = lax.ppermute(u_nxt, "rep", up)
     g_near = lax.ppermute(g_prv, "rep", down)
     pos = after(pos, g_nxt, u_nxt, g_prv, u_prv)
+    x_near, x_far = call(
+        token_kernel,
+        (steps,),
+        [
+            full(2 * count, total // 2),
+            full(2 * count, total // 2),
+            pl.BlockSpec((nodes, 1, 2 * CAP, wcol), lambda i, p: (0, p[2], 0, i)),
+            pl.BlockSpec((nodes, 1, 2 * CAP, wcol), lambda i, p: (0, 1 - p[2], 0, i)),
+        ],
+        [pl.BlockSpec((2 * count, wcol), lambda i, p: (0, i))] * 2,
+        [sds((2 * count, half), BF)] * 2,
+        (pos, keep, got, back, back),
+    )
+    g_far, u_far, x_far = lax.optimization_barrier((g_far, u_far, x_far))
+    x_far = lax.ppermute(x_far, "zlo", swap)
     g_sum = lax.ppermute(add(g_nxt, g_far), "rep", up)
     u_sum = lax.ppermute(add(u_prv, u_far), "rep", down)
 
     own_d = down_part(pos, 0, F32, 1)[0]
     own_g, own_u = gate_up_part(pos, 0, F32)
 
-    x_mine, x_other = call(
-        token_kernel,
-        (steps,),
-        [full(2 * count, total), out_col],
-        [pl.BlockSpec((count, wcol), lambda i, p: (0, i))] * 2,
-        [sds((count, half), BF)] * 2,
-        (pos, sel_t, back),
-    )
+    x_both = (x_near.astype(F32) + x_far.astype(F32)).astype(BF)
+    x_mine, x_other = x_both[:count], x_both[count:]
     x_got = lax.ppermute(x_other, "pair", swap)
     first = core == 0
     x_grad = jnp.concatenate(
@@ -361,16 +380,20 @@
 
 
 def solution(mesh):
-    rows = P(("pair", "wide", "rep"), None)
+    axes = ("pair", "y", "x", "zlo", "rep")
+    pairs, wide, reps = mesh.devices.shape
+    cut = Mesh(mesh.devices.reshape(pairs, 4, wide // 8, 2, reps), axes)
+    rows = P(axes, None)
+    experts = ("y", "x", "zlo")
     in_specs = (rows, rows, rows, rows) + (
-        P("wide", None, "pair"),
-        P("wide", None, "pair"),
-        P("wide", "pair", None),
+        P(experts, None, "pair"),
+        P(experts, None, "pair"),
+        P(experts, "pair", None),
     )
     out_specs = (
         rows,
-        P("wide", "rep", "pair"),
-        P("wide", "rep", "pair"),
-        P("wide", "pair", "rep"),
-    )
-    return jax.shard_map(body, mesh=mesh, in_specs=in_specs, out_specs=out_specs, check_vma=False)
+        P(experts, "rep", "pair"),
+        P(experts, "rep", "pair"),
+        P(experts, "pair", "rep"),
+    )
+    return jax.shard_map(body, mesh=cut, in_specs=in_specs, out_specs=out_specs, check_vma=False)

time: 228 us -> 224 us (0.982)
  waiting for transfers between devices: 72.1 us -> 58.4 us
  starting transfers between devices: 41.8 us -> 48.2 us
  other arithmetic: 8.42 us -> 10.8 us
    ppermute x1, waiting for transfers between devices: 49.3 us -> 0.01 us  [body(): u_far = lax.ppermute(u_far, 'rep', down)]
    ppermute x0 -> x2, waiting for transfers between devices: none -> 24.2 us  [the longest x1 24.2 us: body(): x_far = lax.ppermute(x_far, 'zlo', swap)]
    ppermute x0 -> x2, starting transfers between devices: none -> 13.6 us  [the longest x1 12.4 us: body(): x_far = lax.ppermute(x_far, 'zlo', swap)]
    ppermute x1, starting transfers between devices: 0.86 us -> 5.63 us  [body(): g_far = lax.ppermute(g_far, 'rep', up)]
    all_to_all x1, starting transfers between devices: 9.12 us -> 4.42 us  [body(): lax.all_to_all(row_grad.reshape(nodes, 4 * CAP, half), plane, split_axis=...]
    all_to_all x1, waiting for transfers between devices: 0.01 us -> 4.62 us  [body(): lax.all_to_all(row_grad.reshape(nodes, 4 * CAP, half), plane, split_axis=...]
    ppermute x1, waiting for transfers between devices: 7.66 us -> 12.1 us  [body(): u_sum = lax.ppermute(add(u_prv, u_far), 'rep', down)]
    ppermute x1, starting transfers between devices: 3.59 us -> 0.67 us  [body(): x_got = lax.ppermute(x_other, 'pair', swap)]
  transfers between devices with their start and end apart: 21 -> 23, of which waited for: 8 -> 8; matrix products, arithmetic and copies ran while one was open for 3% -> 4% of each run, Pallas kernels for 13% -> 14%
where the time goes in v2:
time: 224 us; the launch traced here: 223 us
  waiting for transfers between devices  58.4 us (26%)
  blocking collectives  55.1 us (25%)
  starting transfers between devices  48.2 us (22%)
  Pallas kernels  41.3 us (18%)
  other arithmetic  10.8 us (5%)
  local copies, waits for them, and re-layouts  8.15 us (4%)
    all_to_all x1, blocking collectives, body(): lax.all_to_all(sent, experts, split_axis=0, concat_axis=0, tiled=True)  55.1 us
    pallas_call x15, Pallas kernels, call(): pl.pallas_call(kernel, grid_spec=spec, out_shape=out_shape, compiler_para...  41.3 us
    ppermute x1, waiting for transfers between devices, body(): x_far = lax.ppermute(x_far, 'zlo', swap)  24.2 us
    ppermute x1, starting transfers between devices, body(): x_far = lax.ppermute(x_far, 'zlo', swap)  12.4 us
    ppermute x1, waiting for transfers between devices, body(): u_sum = lax.ppermute(add(u_prv, u_far), 'rep', down)  12.1 us
    ppermute x1, waiting for transfers between devices, body(): d_sum_u = lax.ppermute(add(nxt[0], d_far_u), 'rep', up)  8.47 us
    unnamed x66, local copies, waits for them, and re-layouts  7.88 us
    broadcast_in_dim x3, other arithmetic, body(): return (x_grad, gate_grad[None], up_grad[None], down_grad[None])  6.6 us
  transfers between devices with their start and end apart: 23, of which 8 were waited for; matrix products, arithmetic and copies ran while one was open for 4% of the time, Pallas kernels for 14%

profile of v2, /device:TPU:33, one launch (start us, length us, event | category | flops | bytes accessed | tf_op | source)
XLA Modules:
  0.0 223.0 jit_solution(278216605815578389)
XLA Ops:
  0.6 0.8 collective-permute-start.2
  1.4 0.1 collective-permute-start.3
  1.5 0.4 collective-permute-start
  1.9 0.1 collective-permute-start.1
  2.0 0.6 pad_add_fusion.pos
  2.6 1.7 collective-permute-done.ids_b
  4.3 0.6 copy-done.30
  4.9 0.3 copy-done.20
  5.1 0.8 copy-done.21
  6.0 6.6 %shard_map.102 = (bf16[32,2,24,1280]{3,2,1,0:T(8,128)(2,1)}, bf16[256,384]{1,0:T(8,128)(2,1)}, bf16[256,384]{1,0:T(8,128)(2,1)}) custom-call(s32[3]{0:T(128)} %pad_add_fusion.pos, s32[6,128]{1,0:T(8,128)} %bitcast.42, s32[6,128]{1,0:T(8,128)} %copy-done.30, f32[6,128]{1,0:T(8,128)} %bitcast.44, f32[6,128]{1,0:T(8,128)} %copy-done.31, ...), custom_call_target="tpu_custom_call" | custom-call | flops 1 | bytes 1 | tf_op jit(solution)/shard_map/pallas_call | solution.py:28
  12.6 55.1 %all_to_all.10 = bf16[32,2,24,1280]{3,2,1,0:T(8,128)(2,1)S(1)} all-to-all(bf16[32,2,24,1280]{3,2,1,0:T(8,128)(2,1)} %get-tuple-element.51), channel_id=1, replica_groups=mesh['pair'=2,'y'=4,'x'=4,'zlo'=2,'rep'=4] {'y','x','zlo'}, dimensions={0} | all-to-all | bytes 7864320 | tf_op jit(solution)/shard_map/all_to_all | solution.py:225
  67.7 0.3 fusion.1
  68.0 1.7 collective-permute-start.4
  69.7 0.1 collective-permute-start.6
  69.8 1.2 collective-permute-start.5
  71.0 2.8 %shard_map.103 = (bf16[2560,384]{1,0:T(8,128)(2,1)S(1)}, bf16[2560,768]{1,0:T(8,128)(2,1)S(1)}, bf16[768,2560]{1,0:T(8,128)(2,1)S(1)}) custom-call(s32[3]{0:T(128)S(1)} %copy-done.17, bf16[384,2560]{1,0:T(8,128)(2,1)S(1)} %bitcast.38, bf16[2560,384]{1,0:T(8,128)(2,1)S(1)} %bitcast.39, bf16[2560,384]{1,0:T(8,128)(2,1)S(1)} %bitcast.40), custom_call_target="tpu_custom_call" | custom-call | flops 1 | bytes 1 | tf_op jit(solution)/shard_map/pallas_call | solution.py:28
  73.8 4.9 %shard_map.104 = (bf16[2,1280,768]{2,1,0:T(8,128)(2,1)S(1)}, bf16[384,768]{1,0:T(8,128)(2,1)S(1)}, f32[768,768]{1,0:T(8,128)S(1)}) custom-call(s32[3]{0:T(128)S(1)} %copy-done.17, bf16[768,1280]{1,0:T(8,128)(2,1)S(1)} %bitcast.37, bf16[768,1280]{1,0:T(8,128)(2,1)S(1)} %collective-permute-done.4.x_b, bf16[2,1280,768]{2,1,0:T(8,128)(2,1)S(1)} %bitcast.31, ...), custom_call_target="tpu_custom_call" | custom-call | flops 1 | bytes 1 | tf_op jit(solution)/shard_map/pallas_call | solution.py:28
  78.8 1.3 shard_map.105
  80.1 3.1 %collective-permute-start.7 = (bf16[192,640]{1,0:T(8,128)(2,1)S(1)}, bf16[192,640]{1,0:T(8,128)(2,1)S(1)}, u32[]{:S(2)}, u32[]{:S(2)}) collective-permute-start(bf16[192,640]{1,0:T(8,128)(2,1)S(1)} %get-tuple-element.59), channel_id=1, source_target_pairs={{0,1},{1,2},{2,3},{3,0},{4,5},{5,6},{6,7},{7,4},{8,9},{9,10},{10,1... | collective-permute-start | bytes 737288 | tf_op jit(solution)/shard_map/ppermute | solution.py:288
  83.2 2.2 collective-permute-start.8
  85.4 1.3 shard_map.107
  86.8 1.5 shard_map.106
  88.3 3.1 %shard_map.108.backs = bf16[768,768]{1,0:T(8,128)(2,1)S(1)} custom-call(s32[3]{0:T(128)S(1)} %copy-done.17, bf16[768,1280]{1,0:T(8,128)(2,1)S(1)} %bitcast.25, bf16[768,1280]{1,0:T(8,128)(2,1)S(1)} %collective-permute-done.6.g_b, bf16[2,1280,384]{2,1,0:T(8,128)(2,1)S(1)} %bitcast.34, bf16[2,1280,384]{2,1,0:T(8,128)(2,1)S(1)} %bitcast.35, ...), custom_call_target="tpu_custom_call" | custom-call | flops 1 | bytes 1 | tf_op jit(solution)/shard_map/pallas_call | solution.py:28
  91.5 5.1 %collective-permute-done.7 = bf16[192,640]{1,0:T(8,128)(2,1)S(1)} collective-permute-done((bf16[192,640]{1,0:T(8,128)(2,1)S(1)}, bf16[192,640]{1,0:T(8,128)(2,1)S(1)}, u32[]{:S(2)}, u32[]{:S(2)}) %collective-permute-start.7) | collective-permute-done | bytes 245792 | tf_op jit(solution)/shard_map/ppermute | solution.py:288
  96.6 2.8 %shard_map.109 = bf16[768,1280]{1,0:T(8,128)(2,1)S(1)} custom-call(s32[3]{0:T(128)S(1)} %copy-done.17, bf16[768,768]{1,0:T(8,128)(2,1)S(1)} %shard_map.108.backs, bf16[768,2560]{1,0:T(8,128)(2,1)S(1)} %get-tuple-element.69.wgu), custom_call_target="tpu_custom_call" | custom-call | flops 1 | bytes 1 | tf_op jit(solution)/shard_map/pallas_call | solution.py:28
  99.4 1.0 collective-permute-start.9
  100.4 2.4 %collective-permute-start.11 = (bf16[192,640]{1,0:T(8,128)(2,1)S(1)}, bf16[192,640]{1,0:T(8,128)(2,1)S(1)}, u32[]{:S(2)}, u32[]{:S(2)}) collective-permute-start(bf16[192,640]{1,0:T(8,128)(2,1)S(1)} %get-tuple-element.64), channel_id=1, source_target_pairs={{0,3},{1,0},{2,1},{3,2},{4,7},{5,4},{6,5},{7,6},{8,11},{9,8},{10,9... | collective-permute-start | bytes 737288 | tf_op jit(solution)/shard_map/ppermute | solution.py:294
  102.8 1.9 collective-permute-start.10
  104.7 1.8 collective-permute-start.13
  106.5 2.0 collective-permute-start.12
  108.5 1.5 shard_map.110
  110.0 2.8 %shard_map.111 = bf16[768,1280]{1,0:T(8,128)(2,1)S(1)} custom-call(s32[3]{0:T(128)S(1)} %copy-done.17, bf16[768,768]{1,0:T(8,128)(2,1)S(1)} %shard_map.108.backs, bf16[768,2560]{1,0:T(8,128)(2,1)S(1)} %get-tuple-element.69.wgu, bf16[768,1280]{1,0:T(8,128)(2,1)S(1)} %collective-permute-done.9.got), custom_call_target="tpu_custom_call" | custom-call | flops 1 | bytes 1 | tf_op jit(solution)/shard_map/pallas_call | solution.py:28
  112.9 1.3 copy-done.7
  114.2 0.4 collective-permute-done.10
  114.6 0.3 copy-done.22
  114.9 1.8 collective-permute-done.13
  116.7 8.5 %collective-permute-done.12 = bf16[192,640]{1,0:T(8,128)(2,1)S(1)} collective-permute-done((bf16[192,640]{1,0:T(8,128)(2,1)S(1)}, bf16[192,640]{1,0:T(8,128)(2,1)S(1)}, u32[]{:S(2)}, u32[]{:S(2)}) %collective-permute-start.12) | collective-permute-done | bytes 245792 | tf_op jit(solution)/shard_map/ppermute | solution.py:306
  125.2 0.7 copy-done.28
  125.9 4.4 %all-to-all-start.1 = ((bf16[16,48,1280]{2,1,0:T(8,128)(2,1)}), bf16[16,48,1280]{2,1,0:T(8,128)(2,1)}, u32[]{:S(2)}, u32[]{:S(2)}) async-start(bf16[16,48,1280]{2,1,0:T(8,128)(2,1)} %bitcast.33), calls=%async_computation.1 | async-start | bytes 3932160 | tf_op jit(solution)/shard_map/all_to_all | solution.py:335
  130.3 5.6 %collective-permute-start.14 = (bf16[640,384]{1,0:T(8,128)(2,1)}, bf16[640,384]{1,0:T(8,128)(2,1)}, u32[]{:S(2)}, u32[]{:S(2)}) collective-permute-start(bf16[640,384]{1,0:T(8,128)(2,1)} %copy-done.19), channel_id=1, source_target_pairs={{0,1},{1,2},{2,3},{3,0},{4,5},{5,6},{6,7},{7,4},{8,9},{9,10},{10,1... | collective-permute-start | bytes 1474568 | tf_op jit(solution)/shard_map/ppermute | solution.py:338
  135.9 2.1 copy-done.1
  138.0 2.2 %shard_map.113 = (bf16[640,384]{1,0:T(8,128)(2,1)}, bf16[640,384]{1,0:T(8,128)(2,1)S(1)}) custom-call(s32[3]{0:T(128)S(1)} %copy-done.17, bf16[2560,768]{1,0:T(8,128)(2,1)S(1)} %bitcast.28, bf16[768,768]{1,0:T(8,128)(2,1)S(1)} %shard_map.108.backs), custom_call_target="tpu_custom_call" | custom-call | flops 1 | bytes 1 | tf_op jit(solution)/shard_map/pallas_call | solution.py:28
  140.3 0.8 copy-done.14
  141.1 2.2 %shard_map.112 = (bf16[640,384]{1,0:T(8,128)(2,1)S(1)}, bf16[640,384]{1,0:T(8,128)(2,1)}) custom-call(s32[3]{0:T(128)S(1)} %copy-done.17, bf16[2560,768]{1,0:T(8,128)(2,1)S(1)} %bitcast.29, bf16[768,768]{1,0:T(8,128)(2,1)S(1)} %shard_map.108.backs), custom_call_target="tpu_custom_call" | custom-call | flops 1 | bytes 1 | tf_op jit(solution)/shard_map/pallas_call | solution.py:28
  143.3 2.4 %collective-permute-start.21 = (bf16[640,384]{1,0:T(8,128)(2,1)}, bf16[640,384]{1,0:T(8,128)(2,1)}, u32[]{:S(2)}, u32[]{:S(2)}) collective-permute-start(bf16[640,384]{1,0:T(8,128)(2,1)} %get-tuple-element.79), channel_id=1, source_target_pairs={{0,1},{1,2},{2,3},{3,0},{4,5},{5,6},{6,7},{7,4},{8,9},{9,10},{10,1... | collective-permute-start | bytes 1474568 | tf_op jit(solution)/shard_map/ppermute | solution.py:342
  145.7 1.2 collective-permute-start.19
  146.9 1.6 shard_map.116
  148.5 0.9 copy-done.8
  149.5 0.1 convert_add_fusion
  149.6 4.6 %all-to-all-done.1 = bf16[16,48,1280]{2,1,0:T(8,128)(2,1)} async-done(((bf16[16,48,1280]{2,1,0:T(8,128)(2,1)}), bf16[16,48,1280]{2,1,0:T(8,128)(2,1)}, u32[]{:S(2)}, u32[]{:S(2)}) %all-to-all-start.1) | async-done | bytes 1966112 | tf_op jit(solution)/shard_map/all_to_all | solution.py:335
  154.2 5.0 %shard_map.114 = (bf16[256,1280]{1,0:T(8,128)(2,1)S(1)}, bf16[256,1280]{1,0:T(8,128)(2,1)S(1)}) custom-call(s32[3]{0:T(128)S(1)} %copy-done.17, bf16[256,384]{1,0:T(8,128)(2,1)S(1)} %copy-done.16, bf16[256,384]{1,0:T(8,128)(2,1)S(1)} %collective-permute-done.5.got, bf16[16,2,24,1280]{3,2,1,0:T(8,128)(2,1)} %bitcast.14.rows_keep.rows_got, ...), custom_call_target="tpu_custom_call" | custom-call | flops 1 | bytes 1 | tf_op jit(solution)/shard_map/pallas_call | solution.py:28
  159.2 12.4 %collective-permute-start.16 = (bf16[256,1280]{1,0:T(8,128)(2,1)S(1)}, bf16[256,1280]{1,0:T(8,128)(2,1)S(1)}, u32[]{:S(2)}, u32[]{:S(2)}) collective-permute-start(bf16[256,1280]{1,0:T(8,128)(2,1)S(1)} %get-tuple-element.89), channel_id=1, source_target_pairs={{0,4},{4,0},{1,5},{5,1},{2,6},{6,2},{3,7},{7,3},{8,12},{12,8},{9,1... | collective-permute-start | bytes 1966088 | tf_op jit(solution)/shard_map/ppermute | solution.py:359
  171.6 2.3 %fusion = f32[1,384,640]{2,1,0:T(8,128)} fusion(f32[384,640]{1,0:T(8,128)} %copy-done.8, f32[192,640]{1,0:T(8,128)S(1)} %get-tuple-element.102, f32[192,640]{1,0:T(8,128)S(1)} %get-tuple-element.103), kind=kLoop, calls=%fused_computation.2 | loop fusion | flops 491520 | bytes 2949120 | tf_op jit(solution)/shard_map/broadcast_in_dim | solution.py:379
  173.9 1.5 shard_map.115
  175.4 1.2 add_convert_fusion.1
  176.6 2.7 %collective-permute-start.20 = (bf16[640,384]{1,0:T(8,128)(2,1)S(1)}, bf16[640,384]{1,0:T(8,128)(2,1)S(1)}, u32[]{:S(2)}, u32[]{:S(2)}) collective-permute-start(bf16[640,384]{1,0:T(8,128)(2,1)S(1)} %add_convert_fusion.1), channel_id=1, source_target_pairs={{0,3},{1,0},{2,1},{3,2},{4,7},{5,4},{6,5},{7,6},{8,11},{9,8},{10,9... | collective-permute-start | bytes 1474568 | tf_op jit(solution)/shard_map/ppermute | solution.py:361
  179.3 1.2 add_convert_fusion.2
  180.5 24.2 %collective-permute-done.16 = bf16[256,1280]{1,0:T(8,128)(2,1)S(1)} collective-permute-done((bf16[256,1280]{1,0:T(8,128)(2,1)S(1)}, bf16[256,1280]{1,0:T(8,128)(2,1)S(1)}, u32[]{:S(2)}, u32[]{:S(2)}) %collective-permute-start.16) | collective-permute-done | bytes 655392 | tf_op jit(solution)/shard_map/ppermute | solution.py:359
  204.8 0.2 add_convert_fusion
  205.0 0.7 collective-permute-start.17
  205.6 12.1 %collective-permute-done.20 = bf16[640,384]{1,0:T(8,128)(2,1)S(1)} collective-permute-done((bf16[640,384]{1,0:T(8,128)(2,1)S(1)}, bf16[640,384]{1,0:T(8,128)(2,1)S(1)}, u32[]{:S(2)}, u32[]{:S(2)}) %collective-permute-start.20) | collective-permute-done | bytes 491552 | tf_op jit(solution)/shard_map/ppermute | solution.py:361
  217.7 2.2 add_bitcast_fusion
  219.9 2.2 add_bitcast_fusion.1
  222.1 0.9 pad_maximum_fusion
  (78 shorter events, 0.4 us)
Async XLA Ops:
  0.6 3.7 %collective-permute-start.2 = (bf16[128,2560]{1,0:T(8,128)(2,1)}, bf16[128,2560]{1,0:T(8,128)(2,1)S(1)}, u32[]{:S(2)}, u32[]{:S(2)}) collective-permute-start(bf16[128,2560]{1,0:T(8,128)(2,1)} %tok_a.1), channel_id=1, source_target_pairs={{0,128},{128,0},{1,129},{129,1},{2,130},{130,2},{3,131},{131,3},{4... | collective-permute-start | bytes 1966088 | tf_op jit(solution)/shard_map/ppermute | solution.py:182
  1.4 2.9 %collective-permute-start.3 = (bf16[128,2560]{1,0:T(8,128)(2,1)}, bf16[128,2560]{1,0:T(8,128)(2,1)S(1)}, u32[]{:S(2)}, u32[]{:S(2)}) collective-permute-start(bf16[128,2560]{1,0:T(8,128)(2,1)} %og_a.1), channel_id=1, source_target_pairs={{0,128},{128,0},{1,129},{129,1},{2,130},{130,2},{3,131},{131,3},{4... | collective-permute-start | bytes 1966088 | tf_op jit(solution)/shard_map/ppermute | solution.py:183
  1.5 2.8 %collective-permute-start = (s32[6,128]{1,0:T(8,128)}, s32[6,128]{1,0:T(8,128)S(1)}, u32[]{:S(2)}, u32[]{:S(2)}) collective-permute-start(s32[6,128]{1,0:T(8,128)} %bitcast.41), channel_id=1, source_target_pairs={{0,128},{128,0},{1,129},{129,1},{2,130},{130,2},{3,131},{131,3},{4... | collective-permute-start | bytes 9224 | tf_op jit(solution)/shard_map/ppermute | solution.py:180
  1.9 2.4 %collective-permute-start.1 = (f32[6,128]{1,0:T(8,128)}, f32[6,128]{1,0:T(8,128)S(1)}, u32[]{:S(2)}, u32[]{:S(2)}) collective-permute-start(f32[6,128]{1,0:T(8,128)} %bitcast.43), channel_id=1, source_target_pairs={{0,128},{128,0},{1,129},{129,1},{2,130},{130,2},{3,131},{131,3},{4... | collective-permute-start | bytes 9224 | tf_op jit(solution)/shard_map/ppermute | solution.py:181
  4.3 0.6 copy-start.30
  4.3 0.6 copy-start.31
  4.3 0.8 copy-start.20
  5.1 0.8 copy-start.21
  67.7 2.1 copy-start.32
  67.7 3.3 %copy-start.9 = (bf16[1,384,2560]{2,1,0:T(8,128)(2,1)S(1)}, bf16[1,384,2560]{2,1,0:T(8,128)(2,1)}, u32[]{:S(2)}) copy-start(bf16[1,384,2560]{2,1,0:T(8,128)(2,1)} %param.13) | copy-start | bytes 5898244
  67.7 3.3 %copy-start.10 = (bf16[1,2560,384]{2,1,0:T(8,128)(2,1)S(1)}, bf16[1,2560,384]{2,1,0:T(8,128)(2,1)}, u32[]{:S(2)}) copy-start(bf16[1,2560,384]{2,1,0:T(8,128)(2,1)} %param.11) | copy-start | bytes 5898244
  67.7 3.3 %copy-start.11 = (bf16[1,2560,384]{2,1,0:T(8,128)(2,1)S(1)}, bf16[1,2560,384]{2,1,0:T(8,128)(2,1)}, u32[]{:S(2)}) copy-start(bf16[1,2560,384]{2,1,0:T(8,128)(2,1)} %param.12) | copy-start | bytes 5898244
  67.7 3.3 %copy-start.17 = (s32[3]{0:T(128)S(1)}, s32[3]{0:T(128)}, u32[]{:S(2)}) copy-start(s32[3]{0:T(128)} %pad_add_fusion.pos) | copy-start | bytes 40
  68.0 5.8 %collective-permute-start.4 = (bf16[768,1280]{1,0:T(8,128)(2,1)S(1)}, bf16[768,1280]{1,0:T(8,128)(2,1)S(1)}, u32[]{:S(2)}, u32[]{:S(2)}) collective-permute-start(bf16[768,1280]{1,0:T(8,128)(2,1)S(1)} %bitcast.36), channel_id=1, source_target_pairs={{0,128},{128,0},{1,129},{129,1},{2,130},{130,2},{3,131},{131,3},{4... | collective-permute-start | bytes 5898248 | tf_op jit(solution)/shard_map/ppermute | solution.py:229
  69.7 9.1 %collective-permute-start.6 = (bf16[768,1280]{1,0:T(8,128)(2,1)S(1)}, bf16[768,1280]{1,0:T(8,128)(2,1)S(1)}, u32[]{:S(2)}, u32[]{:S(2)}) collective-permute-start(bf16[768,1280]{1,0:T(8,128)(2,1)S(1)} %bitcast.21), channel_id=1, source_target_pairs={{0,128},{128,0},{1,129},{129,1},{2,130},{130,2},{3,131},{131,3},{4... | collective-permute-start | bytes 5898248 | tf_op jit(solution)/shard_map/ppermute | solution.py:258
  69.8 8.9 %collective-permute-start.5 = (bf16[256,384]{1,0:T(8,128)(2,1)S(1)}, bf16[256,384]{1,0:T(8,128)(2,1)S(1)}, u32[]{:S(2)}, u32[]{:S(2)}) collective-permute-start(bf16[256,384]{1,0:T(8,128)(2,1)S(1)} %copy-done.32), channel_id=1, source_target_pairs={{0,4},{4,0},{1,5},{5,1},{2,6},{6,2},{3,7},{7,3},{8,12},{12,8},{9,1... | collective-permute-start | bytes 589832 | tf_op jit(solution)/shard_map/ppermute | solution.py:228
  78.7 8.0 %copy-start.5 = (bf16[384,768]{1,0:T(8,128)(2,1)}, bf16[384,768]{1,0:T(8,128)(2,1)S(1)}, u32[]{:S(2)}) copy-start(bf16[384,768]{1,0:T(8,128)(2,1)S(1)} %get-tuple-element.56.hidden_t) | copy-start | bytes 1769476
  78.7 29.8 %copy-start = (bf16[2,1280,768]{2,1,0:T(8,128)(2,1)}, bf16[2,1280,768]{2,1,0:T(8,128)(2,1)S(1)}, u32[]{:S(2)}) copy-start(bf16[2,1280,768]{2,1,0:T(8,128)(2,1)S(1)} %get-tuple-element.71) | copy-start | bytes 11796484
  78.8 9.6 %copy-start.3 = (bf16[768,1280]{1,0:T(8,128)(2,1)}, bf16[768,1280]{1,0:T(8,128)(2,1)S(1)}, u32[]{:S(2)}) copy-start(bf16[768,1280]{1,0:T(8,128)(2,1)S(1)} %collective-permute-done.6.g_b) | copy-start | bytes 5898244
  80.1 16.4 %collective-permute-start.7 = (bf16[192,640]{1,0:T(8,128)(2,1)S(1)}, bf16[192,640]{1,0:T(8,128)(2,1)S(1)}, u32[]{:S(2)}, u32[]{:S(2)}) collective-permute-start(bf16[192,640]{1,0:T(8,128)(2,1)S(1)} %get-tuple-element.59), channel_id=1, source_target_pairs={{0,1},{1,2},{2,3},{3,0},{4,5},{5,6},{6,7},{7,4},{8,9},{9,10},{10,1... | collective-permute-start | bytes 737288 | tf_op jit(solution)/shard_map/ppermute | solution.py:288
  83.2 13.4 %collective-permute-start.8 = (bf16[192,640]{1,0:T(8,128)(2,1)S(1)}, bf16[192,640]{1,0:T(8,128)(2,1)S(1)}, u32[]{:S(2)}, u32[]{:S(2)}) collective-permute-start(bf16[192,640]{1,0:T(8,128)(2,1)S(1)} %get-tuple-element.60), channel_id=1, source_target_pairs={{0,3},{1,0},{2,1},{3,2},{4,7},{5,4},{6,5},{7,6},{8,11},{9,8},{10,9... | collective-permute-start | bytes 737288 | tf_op jit(solution)/shard_map/ppermute | solution.py:289
  99.4 10.7 %collective-permute-start.9 = (bf16[768,1280]{1,0:T(8,128)(2,1)S(1)}, bf16[768,1280]{1,0:T(8,128)(2,1)S(1)}, u32[]{:S(2)}, u32[]{:S(2)}) collective-permute-start(bf16[768,1280]{1,0:T(8,128)(2,1)S(1)} %shard_map.109), channel_id=1, source_target_pairs={{0,128},{128,0},{1,129},{129,1},{2,130},{130,2},{3,131},{131,3},{4... | collective-permute-start | bytes 5898248 | tf_op jit(solution)/shard_map/ppermute | solution.py:319
  100.4 13.8 %collective-permute-start.11 = (bf16[192,640]{1,0:T(8,128)(2,1)S(1)}, bf16[192,640]{1,0:T(8,128)(2,1)S(1)}, u32[]{:S(2)}, u32[]{:S(2)}) collective-permute-start(bf16[192,640]{1,0:T(8,128)(2,1)S(1)} %get-tuple-element.64), channel_id=1, source_target_pairs={{0,3},{1,0},{2,1},{3,2},{4,7},{5,4},{6,5},{7,6},{8,11},{9,8},{10,9... | collective-permute-start | bytes 737288 | tf_op jit(solution)/shard_map/ppermute | solution.py:294
  102.8 11.9 %collective-permute-start.10 = (bf16[192,640]{1,0:T(8,128)(2,1)S(1)}, bf16[192,640]{1,0:T(8,128)(2,1)S(1)}, u32[]{:S(2)}, u32[]{:S(2)}) collective-permute-start(bf16[192,640]{1,0:T(8,128)(2,1)S(1)} %get-tuple-element.63), channel_id=1, source_target_pairs={{0,1},{1,2},{2,3},{3,0},{4,5},{5,6},{6,7},{7,4},{8,9},{9,10},{10,1... | collective-permute-start | bytes 737288 | tf_op jit(solution)/shard_map/ppermute | solution.py:293
  104.7 12.0 %collective-permute-start.13 = (bf16[192,640]{1,0:T(8,128)(2,1)S(1)}, bf16[192,640]{1,0:T(8,128)(2,1)S(1)}, u32[]{:S(2)}, u32[]{:S(2)}) collective-permute-start(bf16[192,640]{1,0:T(8,128)(2,1)S(1)} %add_convert_fusion.3), channel_id=1, source_target_pairs={{0,3},{1,0},{2,1},{3,2},{4,7},{5,4},{6,5},{7,6},{8,11},{9,8},{10,9... | collective-permute-start | bytes 737288 | tf_op jit(solution)/shard_map/ppermute | solution.py:307
  106.5 18.6 %collective-permute-start.12 = (bf16[192,640]{1,0:T(8,128)(2,1)S(1)}, bf16[192,640]{1,0:T(8,128)(2,1)S(1)}, u32[]{:S(2)}, u32[]{:S(2)}) collective-permute-start(bf16[192,640]{1,0:T(8,128)(2,1)S(1)} %add_convert_fusion.4), channel_id=1, source_target_pairs={{0,1},{1,2},{2,3},{3,0},{4,5},{5,6},{6,7},{7,4},{8,9},{9,10},{10,1... | collective-permute-start | bytes 737288 | tf_op jit(solution)/shard_map/ppermute | solution.py:306
  110.0 2.9 %copy-start.18 = (bf16[640,384]{1,0:T(8,128)(2,1)}, bf16[640,384]{1,0:T(8,128)(2,1)S(1)}, u32[]{:S(2)}) copy-start(bf16[640,384]{1,0:T(8,128)(2,1)S(1)} %get-tuple-element.87) | copy-start | bytes 1474564
  110.0 2.9 %copy-start.19 = (bf16[640,384]{1,0:T(8,128)(2,1)}, bf16[640,384]{1,0:T(8,128)(2,1)S(1)}, u32[]{:S(2)}) copy-start(bf16[640,384]{1,0:T(8,128)(2,1)S(1)} %get-tuple-element.86) | copy-start | bytes 1474564
  112.9 1.3 copy-start.7
  114.2 0.7 copy-start.22
  114.9 1.8 copy-start.24
  116.7 8.5 %copy-start.26 = (bf16[192,640]{1,0:T(8,128)(2,1)}, bf16[192,640]{1,0:T(8,128)(2,1)S(1)}, u32[]{:S(2)}) copy-start(bf16[192,640]{1,0:T(8,128)(2,1)S(1)} %collective-permute-done.13) | copy-start | bytes 737284
  125.2 0.7 copy-start.28
  125.9 28.4 %all-to-all-start.1 = ((bf16[16,48,1280]{2,1,0:T(8,128)(2,1)}), bf16[16,48,1280]{2,1,0:T(8,128)(2,1)}, u32[]{:S(2)}, u32[]{:S(2)}) async-start(bf16[16,48,1280]{2,1,0:T(8,128)(2,1)} %bitcast.33), calls=%async_computation.1 | async-start | bytes 3932160 | tf_op jit(solution)/shard_map/all_to_all | solution.py:335
  130.3 28.9 %collective-permute-start.14 = (bf16[640,384]{1,0:T(8,128)(2,1)}, bf16[640,384]{1,0:T(8,128)(2,1)}, u32[]{:S(2)}, u32[]{:S(2)}) collective-permute-start(bf16[640,384]{1,0:T(8,128)(2,1)} %copy-done.19), channel_id=1, source_target_pairs={{0,1},{1,2},{2,3},{3,0},{4,5},{5,6},{6,7},{7,4},{8,9},{9,10},{10,1... | collective-permute-start | bytes 1474568 | tf_op jit(solution)/shard_map/ppermute | solution.py:338
  135.9 23.3 %collective-permute-start.15 = (bf16[640,384]{1,0:T(8,128)(2,1)}, bf16[640,384]{1,0:T(8,128)(2,1)}, u32[]{:S(2)}, u32[]{:S(2)}) collective-permute-start(bf16[640,384]{1,0:T(8,128)(2,1)} %copy-done.18), channel_id=1, source_target_pairs={{0,3},{1,0},{2,1},{3,2},{4,7},{5,4},{6,5},{7,6},{8,11},{9,8},{10,9... | collective-permute-start | bytes 1474568 | tf_op jit(solution)/shard_map/ppermute | solution.py:339
  135.9 2.1 copy-start.1
  140.3 0.8 copy-start.14
  141.1 5.8 %copy-start.4 = (bf16[768,1280]{1,0:T(8,128)(2,1)S(1)}, bf16[768,1280]{1,0:T(8,128)(2,1)}, u32[]{:S(2)}) copy-start(bf16[768,1280]{1,0:T(8,128)(2,1)} %copy-done.3) | copy-start | bytes 5898244
  141.1 5.8 %copy-start.6 = (bf16[384,768]{1,0:T(8,128)(2,1)S(1)}, bf16[384,768]{1,0:T(8,128)(2,1)}, u32[]{:S(2)}) copy-start(bf16[384,768]{1,0:T(8,128)(2,1)} %copy-done.5) | copy-start | bytes 1769476
  143.3 5.2 %copy-start.12 = (bf16[640,384]{1,0:T(8,128)(2,1)}, bf16[640,384]{1,0:T(8,128)(2,1)S(1)}, u32[]{:S(2)}) copy-start(bf16[640,384]{1,0:T(8,128)(2,1)S(1)} %get-tuple-element.78) | copy-start | bytes 1474564
  143.3 62.3 %collective-permute-start.21 = (bf16[640,384]{1,0:T(8,128)(2,1)}, bf16[640,384]{1,0:T(8,128)(2,1)}, u32[]{:S(2)}, u32[]{:S(2)}) collective-permute-start(bf16[640,384]{1,0:T(8,128)(2,1)} %get-tuple-element.79), channel_id=1, source_target_pairs={{0,1},{1,2},{2,3},{3,0},{4,5},{5,6},{6,7},{7,4},{8,9},{9,10},{10,1... | collective-permute-start | bytes 1474568 | tf_op jit(solution)/shard_map/ppermute | solution.py:342
  145.7 74.2 %collective-permute-start.19 = (bf16[640,384]{1,0:T(8,128)(2,1)}, bf16[640,384]{1,0:T(8,128)(2,1)}, u32[]{:S(2)}, u32[]{:S(2)}) collective-permute-start(bf16[640,384]{1,0:T(8,128)(2,1)} %get-tuple-element.80), channel_id=1, source_target_pairs={{0,3},{1,0},{2,1},{3,2},{4,7},{5,4},{6,5},{7,6},{8,11},{9,8},{10,9... | collective-permute-start | bytes 1474568 | tf_op jit(solution)/shard_map/ppermute | solution.py:343
  146.9 2.6 %copy-start.23 = (bf16[192,640]{1,0:T(8,128)(2,1)S(1)}, bf16[192,640]{1,0:T(8,128)(2,1)}, u32[]{:S(2)}) copy-start(bf16[192,640]{1,0:T(8,128)(2,1)} %copy-done.22) | copy-start | bytes 737284
  146.9 2.6 %copy-start.25 = (bf16[192,640]{1,0:T(8,128)(2,1)S(1)}, bf16[192,640]{1,0:T(8,128)(2,1)}, u32[]{:S(2)}) copy-start(bf16[192,640]{1,0:T(8,128)(2,1)} %copy-done.24) | copy-start | bytes 737284
  146.9 2.6 %copy-start.27 = (bf16[192,640]{1,0:T(8,128)(2,1)S(1)}, bf16[192,640]{1,0:T(8,128)(2,1)}, u32[]{:S(2)}) copy-start(bf16[192,640]{1,0:T(8,128)(2,1)} %copy-done.26) | copy-start | bytes 737284
  146.9 2.5 %copy-start.29 = (bf16[192,640]{1,0:T(8,128)(2,1)S(1)}, bf16[192,640]{1,0:T(8,128)(2,1)}, u32[]{:S(2)}) copy-start(bf16[192,640]{1,0:T(8,128)(2,1)} %copy-done.28) | copy-start | bytes 737284
  148.5 0.9 copy-start.8
  149.5 4.7 %copy-start.16 = (bf16[256,384]{1,0:T(8,128)(2,1)S(1)}, bf16[256,384]{1,0:T(8,128)(2,1)}, u32[]{:S(2)}) copy-start(bf16[256,384]{1,0:T(8,128)(2,1)} %get-tuple-element.83.keep) | copy-start | bytes 589828
  154.2 19.7 %copy-start.2 = (bf16[2,1280,768]{2,1,0:T(8,128)(2,1)S(1)}, bf16[2,1280,768]{2,1,0:T(8,128)(2,1)}, u32[]{:S(2)}) copy-start(bf16[2,1280,768]{2,1,0:T(8,128)(2,1)} %copy-done) | copy-start | bytes 11796484
  159.2 45.5 %collective-permute-start.16 = (bf16[256,1280]{1,0:T(8,128)(2,1)S(1)}, bf16[256,1280]{1,0:T(8,128)(2,1)S(1)}, u32[]{:S(2)}, u32[]{:S(2)}) collective-permute-start(bf16[256,1280]{1,0:T(8,128)(2,1)S(1)} %get-tuple-element.89), channel_id=1, source_target_pairs={{0,4},{4,0},{1,5},{5,1},{2,6},{6,2},{3,7},{7,3},{8,12},{12,8},{9,1... | collective-permute-start | bytes 1966088 | tf_op jit(solution)/shard_map/ppermute | solution.py:359
  173.9 1.5 copy-start.15
  173.9 5.4 %copy-start.13 = (bf16[640,384]{1,0:T(8,128)(2,1)S(1)}, bf16[640,384]{1,0:T(8,128)(2,1)}, u32[]{:S(2)}) copy-start(bf16[640,384]{1,0:T(8,128)(2,1)} %copy-done.12) | copy-start | bytes 1474564
  176.6 41.1 %collective-permute-start.20 = (bf16[640,384]{1,0:T(8,128)(2,1)S(1)}, bf16[640,384]{1,0:T(8,128)(2,1)S(1)}, u32[]{:S(2)}, u32[]{:S(2)}) collective-permute-start(bf16[640,384]{1,0:T(8,128)(2,1)S(1)} %add_convert_fusion.1), channel_id=1, source_target_pairs={{0,3},{1,0},{2,1},{3,2},{4,7},{5,4},{6,5},{7,6},{8,11},{9,8},{10,9... | collective-permute-start | bytes 1474568 | tf_op jit(solution)/shard_map/ppermute | solution.py:361
  180.5 39.4 %collective-permute-start.18 = (bf16[640,384]{1,0:T(8,128)(2,1)S(1)}, bf16[640,384]{1,0:T(8,128)(2,1)S(1)}, u32[]{:S(2)}, u32[]{:S(2)}) collective-permute-start(bf16[640,384]{1,0:T(8,128)(2,1)S(1)} %add_convert_fusion.2), channel_id=1, source_target_pairs={{0,1},{1,2},{2,3},{3,0},{4,5},{5,6},{6,7},{7,4},{8,9},{9,10},{10,1... | collective-permute-start | bytes 1474568 | tf_op jit(solution)/shard_map/ppermute | solution.py:360
  205.0 17.1 %collective-permute-start.17 = (bf16[128,1280]{1,0:T(8,128)(2,1)S(1)}, bf16[128,1280]{1,0:T(8,128)(2,1)S(1)}, u32[]{:S(2)}, u32[]{:S(2)}) collective-permute-start(bf16[128,1280]{1,0:T(8,128)(2,1)S(1)} %slice.19), channel_id=1, source_target_pairs={{0,128},{128,0},{1,129},{129,1},{2,130},{130,2},{3,131},{131,3},{4... | collective-permute-start | bytes 983048 | tf_op jit(solution)/shard_map/ppermute | solution.py:368

commit v3 on v2

--- a/solution.py
+++ b/solution.py
@@ -186,15 +186,12 @@
         return lax.optimization_barrier((place, *values))[0]
 
     steps = 5
-    wcol = half // steps
-    tok_spec = pl.BlockSpec((count, wcol), lambda i, p: (0, p[0] * steps + i))
-    out_col = pl.BlockSpec((total, wcol), lambda i, p: (0, i))
     sent, keep, give = call(
         pack_kernel,
-        (steps,),
-        [full(choices, count)] * 4 + [tok_spec] * 4,
+        (1,),
+        [full(choices, count)] * 4 + [pl.BlockSpec((count, half // 1), lambda i, p: (0, p[0] * 1 + i))] * 4,
         [
-            pl.BlockSpec((wide, 2, 2 * CAP, wcol), lambda i, p: (0, 0, 0, i)),
+            pl.BlockSpec((wide, 2, 2 * CAP, half // 1), lambda i, p: (0, 0, 0, i)),
             full(2 * count, total // 2),
             full(2 * count, total // 2),
         ],
@@ -344,14 +341,14 @@
     pos = after(pos, g_nxt, u_nxt, g_prv, u_prv)
     x_near, x_far = call(
         token_kernel,
-        (steps,),
+        (2,),
         [
             full(2 * count, total // 2),
             full(2 * count, total // 2),
-            pl.BlockSpec((nodes, 1, 2 * CAP, wcol), lambda i, p: (0, p[2], 0, i)),
-            pl.BlockSpec((nodes, 1, 2 * CAP, wcol), lambda i, p: (0, 1 - p[2], 0, i)),
+            pl.BlockSpec((nodes, 1, 2 * CAP, half // 2), lambda i, p: (0, p[2], 0, i)),
+            pl.BlockSpec((nodes, 1, 2 * CAP, half // 2), lambda i, p: (0, 1 - p[2], 0, i)),
         ],
-        [pl.BlockSpec((2 * count, wcol), lambda i, p: (0, i))] * 2,
+        [pl.BlockSpec((2 * count, half // 2), lambda i, p: (0, i))] * 2,
         [sds((2 * count, half), BF)] * 2,
         (pos, keep, got, back, back),
     )

time: 224 us -> 222 us (level)
  Pallas kernels: 41.3 us -> 38.2 us
    pallas_call x15, Pallas kernels: 41.3 us -> 38.2 us  [call(): pl.pallas_call(kernel, grid_spec=spec, out_shape=out_shape, compiler_para...]
  transfers between devices with their start and end apart: 23 -> 23, of which waited for: 8 -> 8; matrix products, arithmetic and copies ran while one was open for 4% -> 4% of each run, Pallas kernels for 14% -> 13%
where the time goes in v3:
time: 222 us
  waiting for transfers between devices  58.7 us (26%)
  blocking collectives  55.1 us (25%)
  starting transfers between devices  49.6 us (22%)
  Pallas kernels  38.2 us (17%)
  other arithmetic  10.8 us (5%)
  local copies, waits for them, and re-layouts  8.14 us (4%)
    all_to_all x1, blocking collectives, body(): lax.all_to_all(sent, experts, split_axis=0, concat_axis=0, tiled=True)  55.1 us
    pallas_call x15, Pallas kernels, call(): pl.pallas_call(kernel, grid_spec=spec, out_shape=out_shape, compiler_para...  38.2 us
    ppermute x1, waiting for transfers between devices, body(): x_far = lax.ppermute(x_far, 'zlo', swap)  24.2 us
    ppermute x1, starting transfers between devices, body(): x_far = lax.ppermute(x_far, 'zlo', swap)  14.6 us
    ppermute x1, waiting for transfers between devices, body(): u_sum = lax.ppermute(add(u_prv, u_far), 'rep', down)  11.9 us
    ppermute x1, waiting for transfers between devices, body(): d_sum_u = lax.ppermute(add(nxt[0], d_far_u), 'rep', up)  8.5 us
    unnamed x66, local copies, waits for them, and re-layouts  7.86 us
    broadcast_in_dim x3, other arithmetic, body(): return (x_grad, gate_grad[None], up_grad[None], down_grad[None])  6.6 us
  transfers between devices with their start and end apart: 23, of which 8 were waited for; matrix products, arithmetic and copies ran while one was open for 4% of the time, Pallas kernels for 13%

profile of v3, /device:TPU:33, one launch (start us, length us, event | category | flops | bytes accessed | tf_op | source)
XLA Modules:
  0.0 221.7 jit_solution(5017299994715648705)
XLA Ops:
  0.6 0.8 collective-permute-start.2
  1.4 0.1 collective-permute-start.3
  1.5 0.4 collective-permute-start
  1.9 0.1 collective-permute-start.1
  2.0 0.6 pad_add_fusion.pos
  2.6 1.7 collective-permute-done.ids_b
  4.3 0.6 copy-done.30
  4.9 0.3 copy-done.20
  5.1 0.8 copy-done.21
  6.0 5.3 %shard_map.102 = (bf16[32,2,24,1280]{3,2,1,0:T(8,128)(2,1)}, bf16[256,384]{1,0:T(8,128)(2,1)}, bf16[256,384]{1,0:T(8,128)(2,1)}) custom-call(s32[3]{0:T(128)} %pad_add_fusion.pos, s32[6,128]{1,0:T(8,128)} %bitcast.42, s32[6,128]{1,0:T(8,128)} %copy-done.30, f32[6,128]{1,0:T(8,128)} %bitcast.44, f32[6,128]{1,0:T(8,128)} %copy-done.31, ...), custom_call_target="tpu_custom_call" | custom-call | flops 1 | bytes 1 | tf_op jit(solution)/shard_map/pallas_call | solution.py:28
  11.3 55.1 %all_to_all.10 = bf16[32,2,24,1280]{3,2,1,0:T(8,128)(2,1)S(1)} all-to-all(bf16[32,2,24,1280]{3,2,1,0:T(8,128)(2,1)} %get-tuple-element.51), channel_id=1, replica_groups=mesh['pair'=2,'y'=4,'x'=4,'zlo'=2,'rep'=4] {'y','x','zlo'}, dimensions={0} | all-to-all | bytes 7864320 | tf_op jit(solution)/shard_map/all_to_all | solution.py:222
  66.4 0.3 fusion.1
  66.7 1.7 collective-permute-start.4
  68.4 0.1 collective-permute-start.6
  68.5 1.2 collective-permute-start.5
  69.7 2.8 %shard_map.103 = (bf16[2560,384]{1,0:T(8,128)(2,1)S(1)}, bf16[2560,768]{1,0:T(8,128)(2,1)S(1)}, bf16[768,2560]{1,0:T(8,128)(2,1)S(1)}) custom-call(s32[3]{0:T(128)S(1)} %copy-done.17, bf16[384,2560]{1,0:T(8,128)(2,1)S(1)} %bitcast.38, bf16[2560,384]{1,0:T(8,128)(2,1)S(1)} %bitcast.39, bf16[2560,384]{1,0:T(8,128)(2,1)S(1)} %bitcast.40), custom_call_target="tpu_custom_call" | custom-call | flops 1 | bytes 1 | tf_op jit(solution)/shard_map/pallas_call | solution.py:28
  72.5 4.9 %shard_map.104 = (bf16[2,1280,768]{2,1,0:T(8,128)(2,1)S(1)}, bf16[384,768]{1,0:T(8,128)(2,1)S(1)}, f32[768,768]{1,0:T(8,128)S(1)}) custom-call(s32[3]{0:T(128)S(1)} %copy-done.17, bf16[768,1280]{1,0:T(8,128)(2,1)S(1)} %bitcast.37, bf16[768,1280]{1,0:T(8,128)(2,1)S(1)} %collective-permute-done.4.x_b, bf16[2,1280,768]{2,1,0:T(8,128)(2,1)S(1)} %bitcast.31, ...), custom_call_target="tpu_custom_call" | custom-call | flops 1 | bytes 1 | tf_op jit(solution)/shard_map/pallas_call | solution.py:28
  77.4 1.3 shard_map.105
  78.8 3.1 %collective-permute-start.7 = (bf16[192,640]{1,0:T(8,128)(2,1)S(1)}, bf16[192,640]{1,0:T(8,128)(2,1)S(1)}, u32[]{:S(2)}, u32[]{:S(2)}) collective-permute-start(bf16[192,640]{1,0:T(8,128)(2,1)S(1)} %get-tuple-element.59), channel_id=1, source_target_pairs={{0,1},{1,2},{2,3},{3,0},{4,5},{5,6},{6,7},{7,4},{8,9},{9,10},{10,1... | collective-permute-start | bytes 737288 | tf_op jit(solution)/shard_map/ppermute | solution.py:285
  81.9 2.2 %collective-permute-start.8 = (bf16[192,640]{1,0:T(8,128)(2,1)S(1)}, bf16[192,640]{1,0:T(8,128)(2,1)S(1)}, u32[]{:S(2)}, u32[]{:S(2)}) collective-permute-start(bf16[192,640]{1,0:T(8,128)(2,1)S(1)} %get-tuple-element.60), channel_id=1, source_target_pairs={{0,3},{1,0},{2,1},{3,2},{4,7},{5,4},{6,5},{7,6},{8,11},{9,8},{10,9... | collective-permute-start | bytes 737288 | tf_op jit(solution)/shard_map/ppermute | solution.py:286
  84.1 1.3 shard_map.107
  85.4 1.5 shard_map.106
  87.0 3.1 %shard_map.108.backs = bf16[768,768]{1,0:T(8,128)(2,1)S(1)} custom-call(s32[3]{0:T(128)S(1)} %copy-done.17, bf16[768,1280]{1,0:T(8,128)(2,1)S(1)} %bitcast.25, bf16[768,1280]{1,0:T(8,128)(2,1)S(1)} %collective-permute-done.6.g_b, bf16[2,1280,384]{2,1,0:T(8,128)(2,1)S(1)} %bitcast.34, bf16[2,1280,384]{2,1,0:T(8,128)(2,1)S(1)} %bitcast.35, ...), custom_call_target="tpu_custom_call" | custom-call | flops 1 | bytes 1 | tf_op jit(solution)/shard_map/pallas_call | solution.py:28
  90.1 5.1 %collective-permute-done.7 = bf16[192,640]{1,0:T(8,128)(2,1)S(1)} collective-permute-done((bf16[192,640]{1,0:T(8,128)(2,1)S(1)}, bf16[192,640]{1,0:T(8,128)(2,1)S(1)}, u32[]{:S(2)}, u32[]{:S(2)}) %collective-permute-start.7) | collective-permute-done | bytes 245792 | tf_op jit(solution)/shard_map/ppermute | solution.py:285
  95.2 2.8 %shard_map.109 = bf16[768,1280]{1,0:T(8,128)(2,1)S(1)} custom-call(s32[3]{0:T(128)S(1)} %copy-done.17, bf16[768,768]{1,0:T(8,128)(2,1)S(1)} %shard_map.108.backs, bf16[768,2560]{1,0:T(8,128)(2,1)S(1)} %get-tuple-element.69.wgu), custom_call_target="tpu_custom_call" | custom-call | flops 1 | bytes 1 | tf_op jit(solution)/shard_map/pallas_call | solution.py:28
  98.0 1.0 collective-permute-start.9
  99.0 2.4 %collective-permute-start.11 = (bf16[192,640]{1,0:T(8,128)(2,1)S(1)}, bf16[192,640]{1,0:T(8,128)(2,1)S(1)}, u32[]{:S(2)}, u32[]{:S(2)}) collective-permute-start(bf16[192,640]{1,0:T(8,128)(2,1)S(1)} %get-tuple-element.64), channel_id=1, source_target_pairs={{0,3},{1,0},{2,1},{3,2},{4,7},{5,4},{6,5},{7,6},{8,11},{9,8},{10,9... | collective-permute-start | bytes 737288 | tf_op jit(solution)/shard_map/ppermute | solution.py:291
  101.4 1.9 collective-permute-start.10
  103.4 1.8 collective-permute-start.13
  105.2 2.0 collective-permute-start.12
  107.2 1.5 shard_map.110
  108.7 2.8 %shard_map.111 = bf16[768,1280]{1,0:T(8,128)(2,1)S(1)} custom-call(s32[3]{0:T(128)S(1)} %copy-done.17, bf16[768,768]{1,0:T(8,128)(2,1)S(1)} %shard_map.108.backs, bf16[768,2560]{1,0:T(8,128)(2,1)S(1)} %get-tuple-element.69.wgu, bf16[768,1280]{1,0:T(8,128)(2,1)S(1)} %collective-permute-done.9.got), custom_call_target="tpu_custom_call" | custom-call | flops 1 | bytes 1 | tf_op jit(solution)/shard_map/pallas_call | solution.py:28
  111.5 1.3 copy-done.7
  112.9 0.4 collective-permute-done.10
  113.3 0.3 copy-done.22
  113.6 1.8 collective-permute-done.13
  115.3 8.5 %collective-permute-done.12 = bf16[192,640]{1,0:T(8,128)(2,1)S(1)} collective-permute-done((bf16[192,640]{1,0:T(8,128)(2,1)S(1)}, bf16[192,640]{1,0:T(8,128)(2,1)S(1)}, u32[]{:S(2)}, u32[]{:S(2)}) %collective-permute-start.12) | collective-permute-done | bytes 245792 | tf_op jit(solution)/shard_map/ppermute | solution.py:303
  123.8 0.7 copy-done.28
  124.5 4.4 %all-to-all-start.1 = ((bf16[16,48,1280]{2,1,0:T(8,128)(2,1)}), bf16[16,48,1280]{2,1,0:T(8,128)(2,1)}, u32[]{:S(2)}, u32[]{:S(2)}) async-start(bf16[16,48,1280]{2,1,0:T(8,128)(2,1)} %bitcast.33), calls=%async_computation.1 | async-start | bytes 3932160 | tf_op jit(solution)/shard_map/all_to_all | solution.py:332
  129.0 5.2 %collective-permute-start.14 = (bf16[640,384]{1,0:T(8,128)(2,1)}, bf16[640,384]{1,0:T(8,128)(2,1)}, u32[]{:S(2)}, u32[]{:S(2)}) collective-permute-start(bf16[640,384]{1,0:T(8,128)(2,1)} %copy-done.19), channel_id=1, source_target_pairs={{0,1},{1,2},{2,3},{3,0},{4,5},{5,6},{6,7},{7,4},{8,9},{9,10},{10,1... | collective-permute-start | bytes 1474568 | tf_op jit(solution)/shard_map/ppermute | solution.py:335
  134.2 2.1 copy-done.1
  136.3 2.2 %shard_map.113 = (bf16[640,384]{1,0:T(8,128)(2,1)}, bf16[640,384]{1,0:T(8,128)(2,1)S(1)}) custom-call(s32[3]{0:T(128)S(1)} %copy-done.17, bf16[2560,768]{1,0:T(8,128)(2,1)S(1)} %bitcast.28, bf16[768,768]{1,0:T(8,128)(2,1)S(1)} %shard_map.108.backs), custom_call_target="tpu_custom_call" | custom-call | flops 1 | bytes 1 | tf_op jit(solution)/shard_map/pallas_call | solution.py:28
  138.5 0.8 copy-done.14
  139.3 2.2 %shard_map.112 = (bf16[640,384]{1,0:T(8,128)(2,1)S(1)}, bf16[640,384]{1,0:T(8,128)(2,1)}) custom-call(s32[3]{0:T(128)S(1)} %copy-done.17, bf16[2560,768]{1,0:T(8,128)(2,1)S(1)} %bitcast.29, bf16[768,768]{1,0:T(8,128)(2,1)S(1)} %shard_map.108.backs), custom_call_target="tpu_custom_call" | custom-call | flops 1 | bytes 1 | tf_op jit(solution)/shard_map/pallas_call | solution.py:28
  141.6 2.4 %collective-permute-start.21 = (bf16[640,384]{1,0:T(8,128)(2,1)}, bf16[640,384]{1,0:T(8,128)(2,1)}, u32[]{:S(2)}, u32[]{:S(2)}) collective-permute-start(bf16[640,384]{1,0:T(8,128)(2,1)} %get-tuple-element.79), channel_id=1, source_target_pairs={{0,1},{1,2},{2,3},{3,0},{4,5},{5,6},{6,7},{7,4},{8,9},{9,10},{10,1... | collective-permute-start | bytes 1474568 | tf_op jit(solution)/shard_map/ppermute | solution.py:339
  143.9 1.2 collective-permute-start.19
  145.2 1.6 shard_map.116
  146.8 0.9 copy-done.8
  147.8 5.1 %all-to-all-done.1 = bf16[16,48,1280]{2,1,0:T(8,128)(2,1)} async-done(((bf16[16,48,1280]{2,1,0:T(8,128)(2,1)}), bf16[16,48,1280]{2,1,0:T(8,128)(2,1)}, u32[]{:S(2)}, u32[]{:S(2)}) %all-to-all-start.1) | async-done | bytes 1966112 | tf_op jit(solution)/shard_map/all_to_all | solution.py:332
  152.9 3.2 %shard_map.114 = (bf16[256,1280]{1,0:T(8,128)(2,1)S(1)}, bf16[256,1280]{1,0:T(8,128)(2,1)S(1)}) custom-call(s32[3]{0:T(128)S(1)} %copy-done.17, bf16[256,384]{1,0:T(8,128)(2,1)S(1)} %copy-done.16, bf16[256,384]{1,0:T(8,128)(2,1)S(1)} %collective-permute-done.5.got, bf16[16,2,24,1280]{3,2,1,0:T(8,128)(2,1)} %bitcast.14.rows_keep.rows_got, ...), custom_call_target="tpu_custom_call" | custom-call | flops 1 | bytes 1 | tf_op jit(solution)/shard_map/pallas_call | solution.py:28
  156.2 14.6 %collective-permute-start.16 = (bf16[256,1280]{1,0:T(8,128)(2,1)S(1)}, bf16[256,1280]{1,0:T(8,128)(2,1)S(1)}, u32[]{:S(2)}, u32[]{:S(2)}) collective-permute-start(bf16[256,1280]{1,0:T(8,128)(2,1)S(1)} %get-tuple-element.89), channel_id=1, source_target_pairs={{0,4},{4,0},{1,5},{5,1},{2,6},{6,2},{3,7},{7,3},{8,12},{12,8},{9,1... | collective-permute-start | bytes 1966088 | tf_op jit(solution)/shard_map/ppermute | solution.py:356
  170.8 2.3 %fusion = f32[1,384,640]{2,1,0:T(8,128)} fusion(f32[384,640]{1,0:T(8,128)} %copy-done.8, f32[192,640]{1,0:T(8,128)S(1)} %get-tuple-element.102, f32[192,640]{1,0:T(8,128)S(1)} %get-tuple-element.103), kind=kLoop, calls=%fused_computation.2 | loop fusion | flops 491520 | bytes 2949120 | tf_op jit(solution)/shard_map/broadcast_in_dim | solution.py:376
  173.0 1.5 shard_map.115
  174.5 1.2 add_convert_fusion.1
  175.7 1.3 collective-permute-start.20
  177.0 1.2 add_convert_fusion.2
  178.2 1.2 collective-permute-start.18
  179.4 24.2 %collective-permute-done.16 = bf16[256,1280]{1,0:T(8,128)(2,1)S(1)} collective-permute-done((bf16[256,1280]{1,0:T(8,128)(2,1)S(1)}, bf16[256,1280]{1,0:T(8,128)(2,1)S(1)}, u32[]{:S(2)}, u32[]{:S(2)}) %collective-permute-start.16) | collective-permute-done | bytes 655392 | tf_op jit(solution)/shard_map/ppermute | solution.py:356
  203.6 0.2 add_convert_fusion
  203.8 0.7 collective-permute-start.17
  204.4 11.9 %collective-permute-done.20 = bf16[640,384]{1,0:T(8,128)(2,1)S(1)} collective-permute-done((bf16[640,384]{1,0:T(8,128)(2,1)S(1)}, bf16[640,384]{1,0:T(8,128)(2,1)S(1)}, u32[]{:S(2)}, u32[]{:S(2)}) %collective-permute-start.20) | collective-permute-done | bytes 491552 | tf_op jit(solution)/shard_map/ppermute | solution.py:358
  216.4 2.2 add_bitcast_fusion
  218.6 2.2 add_bitcast_fusion.1
  220.8 0.9 pad_maximum_fusion
  (78 shorter events, 0.5 us)
Async XLA Ops:
  0.6 3.7 %collective-permute-start.2 = (bf16[128,2560]{1,0:T(8,128)(2,1)}, bf16[128,2560]{1,0:T(8,128)(2,1)S(1)}, u32[]{:S(2)}, u32[]{:S(2)}) collective-permute-start(bf16[128,2560]{1,0:T(8,128)(2,1)} %tok_a.1), channel_id=1, source_target_pairs={{0,128},{128,0},{1,129},{129,1},{2,130},{130,2},{3,131},{131,3},{4... | collective-permute-start | bytes 1966088 | tf_op jit(solution)/shard_map/ppermute | solution.py:182
  1.4 2.9 %collective-permute-start.3 = (bf16[128,2560]{1,0:T(8,128)(2,1)}, bf16[128,2560]{1,0:T(8,128)(2,1)S(1)}, u32[]{:S(2)}, u32[]{:S(2)}) collective-permute-start(bf16[128,2560]{1,0:T(8,128)(2,1)} %og_a.1), channel_id=1, source_target_pairs={{0,128},{128,0},{1,129},{129,1},{2,130},{130,2},{3,131},{131,3},{4... | collective-permute-start | bytes 1966088 | tf_op jit(solution)/shard_map/ppermute | solution.py:183
  1.5 2.8 %collective-permute-start = (s32[6,128]{1,0:T(8,128)}, s32[6,128]{1,0:T(8,128)S(1)}, u32[]{:S(2)}, u32[]{:S(2)}) collective-permute-start(s32[6,128]{1,0:T(8,128)} %bitcast.41), channel_id=1, source_target_pairs={{0,128},{128,0},{1,129},{129,1},{2,130},{130,2},{3,131},{131,3},{4... | collective-permute-start | bytes 9224 | tf_op jit(solution)/shard_map/ppermute | solution.py:180
  1.9 2.4 %collective-permute-start.1 = (f32[6,128]{1,0:T(8,128)}, f32[6,128]{1,0:T(8,128)S(1)}, u32[]{:S(2)}, u32[]{:S(2)}) collective-permute-start(f32[6,128]{1,0:T(8,128)} %bitcast.43), channel_id=1, source_target_pairs={{0,128},{128,0},{1,129},{129,1},{2,130},{130,2},{3,131},{131,3},{4... | collective-permute-start | bytes 9224 | tf_op jit(solution)/shard_map/ppermute | solution.py:181
  4.3 0.6 copy-start.30
  4.3 0.6 copy-start.31
  4.3 0.8 copy-start.20
  5.1 0.8 copy-start.21
  66.4 2.1 copy-start.32
  66.4 3.3 %copy-start.9 = (bf16[1,384,2560]{2,1,0:T(8,128)(2,1)S(1)}, bf16[1,384,2560]{2,1,0:T(8,128)(2,1)}, u32[]{:S(2)}) copy-start(bf16[1,384,2560]{2,1,0:T(8,128)(2,1)} %param.13) | copy-start | bytes 5898244
  66.4 3.3 %copy-start.10 = (bf16[1,2560,384]{2,1,0:T(8,128)(2,1)S(1)}, bf16[1,2560,384]{2,1,0:T(8,128)(2,1)}, u32[]{:S(2)}) copy-start(bf16[1,2560,384]{2,1,0:T(8,128)(2,1)} %param.11) | copy-start | bytes 5898244
  66.4 3.3 %copy-start.11 = (bf16[1,2560,384]{2,1,0:T(8,128)(2,1)S(1)}, bf16[1,2560,384]{2,1,0:T(8,128)(2,1)}, u32[]{:S(2)}) copy-start(bf16[1,2560,384]{2,1,0:T(8,128)(2,1)} %param.12) | copy-start | bytes 5898244
  66.4 3.3 %copy-start.17 = (s32[3]{0:T(128)S(1)}, s32[3]{0:T(128)}, u32[]{:S(2)}) copy-start(s32[3]{0:T(128)} %pad_add_fusion.pos) | copy-start | bytes 40
  66.7 5.8 %collective-permute-start.4 = (bf16[768,1280]{1,0:T(8,128)(2,1)S(1)}, bf16[768,1280]{1,0:T(8,128)(2,1)S(1)}, u32[]{:S(2)}, u32[]{:S(2)}) collective-permute-start(bf16[768,1280]{1,0:T(8,128)(2,1)S(1)} %bitcast.36), channel_id=1, source_target_pairs={{0,128},{128,0},{1,129},{129,1},{2,130},{130,2},{3,131},{131,3},{4... | collective-permute-start | bytes 5898248 | tf_op jit(solution)/shard_map/ppermute | solution.py:226
  68.4 9.1 %collective-permute-start.6 = (bf16[768,1280]{1,0:T(8,128)(2,1)S(1)}, bf16[768,1280]{1,0:T(8,128)(2,1)S(1)}, u32[]{:S(2)}, u32[]{:S(2)}) collective-permute-start(bf16[768,1280]{1,0:T(8,128)(2,1)S(1)} %bitcast.21), channel_id=1, source_target_pairs={{0,128},{128,0},{1,129},{129,1},{2,130},{130,2},{3,131},{131,3},{4... | collective-permute-start | bytes 5898248 | tf_op jit(solution)/shard_map/ppermute | solution.py:255
  68.5 8.9 %collective-permute-start.5 = (bf16[256,384]{1,0:T(8,128)(2,1)S(1)}, bf16[256,384]{1,0:T(8,128)(2,1)S(1)}, u32[]{:S(2)}, u32[]{:S(2)}) collective-permute-start(bf16[256,384]{1,0:T(8,128)(2,1)S(1)} %copy-done.32), channel_id=1, source_target_pairs={{0,4},{4,0},{1,5},{5,1},{2,6},{6,2},{3,7},{7,3},{8,12},{12,8},{9,1... | collective-permute-start | bytes 589832 | tf_op jit(solution)/shard_map/ppermute | solution.py:225
  77.4 8.0 %copy-start.5 = (bf16[384,768]{1,0:T(8,128)(2,1)}, bf16[384,768]{1,0:T(8,128)(2,1)S(1)}, u32[]{:S(2)}) copy-start(bf16[384,768]{1,0:T(8,128)(2,1)S(1)} %get-tuple-element.56.hidden_t) | copy-start | bytes 1769476
  77.4 29.8 %copy-start = (bf16[2,1280,768]{2,1,0:T(8,128)(2,1)}, bf16[2,1280,768]{2,1,0:T(8,128)(2,1)S(1)}, u32[]{:S(2)}) copy-start(bf16[2,1280,768]{2,1,0:T(8,128)(2,1)S(1)} %get-tuple-element.71) | copy-start | bytes 11796484
  77.4 9.5 %copy-start.3 = (bf16[768,1280]{1,0:T(8,128)(2,1)}, bf16[768,1280]{1,0:T(8,128)(2,1)S(1)}, u32[]{:S(2)}) copy-start(bf16[768,1280]{1,0:T(8,128)(2,1)S(1)} %collective-permute-done.6.g_b) | copy-start | bytes 5898244
  78.8 16.4 %collective-permute-start.7 = (bf16[192,640]{1,0:T(8,128)(2,1)S(1)}, bf16[192,640]{1,0:T(8,128)(2,1)S(1)}, u32[]{:S(2)}, u32[]{:S(2)}) collective-permute-start(bf16[192,640]{1,0:T(8,128)(2,1)S(1)} %get-tuple-element.59), channel_id=1, source_target_pairs={{0,1},{1,2},{2,3},{3,0},{4,5},{5,6},{6,7},{7,4},{8,9},{9,10},{10,1... | collective-permute-start | bytes 737288 | tf_op jit(solution)/shard_map/ppermute | solution.py:285
  81.9 13.4 %collective-permute-start.8 = (bf16[192,640]{1,0:T(8,128)(2,1)S(1)}, bf16[192,640]{1,0:T(8,128)(2,1)S(1)}, u32[]{:S(2)}, u32[]{:S(2)}) collective-permute-start(bf16[192,640]{1,0:T(8,128)(2,1)S(1)} %get-tuple-element.60), channel_id=1, source_target_pairs={{0,3},{1,0},{2,1},{3,2},{4,7},{5,4},{6,5},{7,6},{8,11},{9,8},{10,9... | collective-permute-start | bytes 737288 | tf_op jit(solution)/shard_map/ppermute | solution.py:286
  98.0 10.6 %collective-permute-start.9 = (bf16[768,1280]{1,0:T(8,128)(2,1)S(1)}, bf16[768,1280]{1,0:T(8,128)(2,1)S(1)}, u32[]{:S(2)}, u32[]{:S(2)}) collective-permute-start(bf16[768,1280]{1,0:T(8,128)(2,1)S(1)} %shard_map.109), channel_id=1, source_target_pairs={{0,128},{128,0},{1,129},{129,1},{2,130},{130,2},{3,131},{131,3},{4... | collective-permute-start | bytes 5898248 | tf_op jit(solution)/shard_map/ppermute | solution.py:316
  99.0 13.8 %collective-permute-start.11 = (bf16[192,640]{1,0:T(8,128)(2,1)S(1)}, bf16[192,640]{1,0:T(8,128)(2,1)S(1)}, u32[]{:S(2)}, u32[]{:S(2)}) collective-permute-start(bf16[192,640]{1,0:T(8,128)(2,1)S(1)} %get-tuple-element.64), channel_id=1, source_target_pairs={{0,3},{1,0},{2,1},{3,2},{4,7},{5,4},{6,5},{7,6},{8,11},{9,8},{10,9... | collective-permute-start | bytes 737288 | tf_op jit(solution)/shard_map/ppermute | solution.py:291
  101.4 11.9 %collective-permute-start.10 = (bf16[192,640]{1,0:T(8,128)(2,1)S(1)}, bf16[192,640]{1,0:T(8,128)(2,1)S(1)}, u32[]{:S(2)}, u32[]{:S(2)}) collective-permute-start(bf16[192,640]{1,0:T(8,128)(2,1)S(1)} %get-tuple-element.63), channel_id=1, source_target_pairs={{0,1},{1,2},{2,3},{3,0},{4,5},{5,6},{6,7},{7,4},{8,9},{9,10},{10,1... | collective-permute-start | bytes 737288 | tf_op jit(solution)/shard_map/ppermute | solution.py:290
  103.4 12.0 %collective-permute-start.13 = (bf16[192,640]{1,0:T(8,128)(2,1)S(1)}, bf16[192,640]{1,0:T(8,128)(2,1)S(1)}, u32[]{:S(2)}, u32[]{:S(2)}) collective-permute-start(bf16[192,640]{1,0:T(8,128)(2,1)S(1)} %add_convert_fusion.3), channel_id=1, source_target_pairs={{0,3},{1,0},{2,1},{3,2},{4,7},{5,4},{6,5},{7,6},{8,11},{9,8},{10,9... | collective-permute-start | bytes 737288 | tf_op jit(solution)/shard_map/ppermute | solution.py:304
  105.2 18.6 %collective-permute-start.12 = (bf16[192,640]{1,0:T(8,128)(2,1)S(1)}, bf16[192,640]{1,0:T(8,128)(2,1)S(1)}, u32[]{:S(2)}, u32[]{:S(2)}) collective-permute-start(bf16[192,640]{1,0:T(8,128)(2,1)S(1)} %add_convert_fusion.4), channel_id=1, source_target_pairs={{0,1},{1,2},{2,3},{3,0},{4,5},{5,6},{6,7},{7,4},{8,9},{9,10},{10,1... | collective-permute-start | bytes 737288 | tf_op jit(solution)/shard_map/ppermute | solution.py:303
  108.7 2.8 %copy-start.18 = (bf16[640,384]{1,0:T(8,128)(2,1)}, bf16[640,384]{1,0:T(8,128)(2,1)S(1)}, u32[]{:S(2)}) copy-start(bf16[640,384]{1,0:T(8,128)(2,1)S(1)} %get-tuple-element.87) | copy-start | bytes 1474564
  108.7 2.8 %copy-start.19 = (bf16[640,384]{1,0:T(8,128)(2,1)}, bf16[640,384]{1,0:T(8,128)(2,1)S(1)}, u32[]{:S(2)}) copy-start(bf16[640,384]{1,0:T(8,128)(2,1)S(1)} %get-tuple-element.86) | copy-start | bytes 1474564
  111.5 1.3 copy-start.7
  112.9 0.7 copy-start.22
  113.6 1.8 copy-start.24
  115.3 8.5 %copy-start.26 = (bf16[192,640]{1,0:T(8,128)(2,1)}, bf16[192,640]{1,0:T(8,128)(2,1)S(1)}, u32[]{:S(2)}) copy-start(bf16[192,640]{1,0:T(8,128)(2,1)S(1)} %collective-permute-done.13) | copy-start | bytes 737284
  123.8 0.7 copy-start.28
  124.5 28.4 %all-to-all-start.1 = ((bf16[16,48,1280]{2,1,0:T(8,128)(2,1)}), bf16[16,48,1280]{2,1,0:T(8,128)(2,1)}, u32[]{:S(2)}, u32[]{:S(2)}) async-start(bf16[16,48,1280]{2,1,0:T(8,128)(2,1)} %bitcast.33), calls=%async_computation.1 | async-start | bytes 3932160 | tf_op jit(solution)/shard_map/all_to_all | solution.py:332
  129.0 27.2 %collective-permute-start.14 = (bf16[640,384]{1,0:T(8,128)(2,1)}, bf16[640,384]{1,0:T(8,128)(2,1)}, u32[]{:S(2)}, u32[]{:S(2)}) collective-permute-start(bf16[640,384]{1,0:T(8,128)(2,1)} %copy-done.19), channel_id=1, source_target_pairs={{0,1},{1,2},{2,3},{3,0},{4,5},{5,6},{6,7},{7,4},{8,9},{9,10},{10,1... | collective-permute-start | bytes 1474568 | tf_op jit(solution)/shard_map/ppermute | solution.py:335
  134.2 22.0 %collective-permute-start.15 = (bf16[640,384]{1,0:T(8,128)(2,1)}, bf16[640,384]{1,0:T(8,128)(2,1)}, u32[]{:S(2)}, u32[]{:S(2)}) collective-permute-start(bf16[640,384]{1,0:T(8,128)(2,1)} %copy-done.18), channel_id=1, source_target_pairs={{0,3},{1,0},{2,1},{3,2},{4,7},{5,4},{6,5},{7,6},{8,11},{9,8},{10,9... | collective-permute-start | bytes 1474568 | tf_op jit(solution)/shard_map/ppermute | solution.py:336
  134.2 2.1 copy-start.1
  138.5 0.8 copy-start.14
  139.3 5.8 %copy-start.4 = (bf16[768,1280]{1,0:T(8,128)(2,1)S(1)}, bf16[768,1280]{1,0:T(8,128)(2,1)}, u32[]{:S(2)}) copy-start(bf16[768,1280]{1,0:T(8,128)(2,1)} %copy-done.3) | copy-start | bytes 5898244
  139.3 5.8 %copy-start.6 = (bf16[384,768]{1,0:T(8,128)(2,1)S(1)}, bf16[384,768]{1,0:T(8,128)(2,1)}, u32[]{:S(2)}) copy-start(bf16[384,768]{1,0:T(8,128)(2,1)} %copy-done.5) | copy-start | bytes 1769476
  141.6 5.2 %copy-start.12 = (bf16[640,384]{1,0:T(8,128)(2,1)}, bf16[640,384]{1,0:T(8,128)(2,1)S(1)}, u32[]{:S(2)}) copy-start(bf16[640,384]{1,0:T(8,128)(2,1)S(1)} %get-tuple-element.78) | copy-start | bytes 1474564
  141.6 62.9 %collective-permute-start.21 = (bf16[640,384]{1,0:T(8,128)(2,1)}, bf16[640,384]{1,0:T(8,128)(2,1)}, u32[]{:S(2)}, u32[]{:S(2)}) collective-permute-start(bf16[640,384]{1,0:T(8,128)(2,1)} %get-tuple-element.79), channel_id=1, source_target_pairs={{0,1},{1,2},{2,3},{3,0},{4,5},{5,6},{6,7},{7,4},{8,9},{9,10},{10,1... | collective-permute-start | bytes 1474568 | tf_op jit(solution)/shard_map/ppermute | solution.py:339
  143.9 74.6 %collective-permute-start.19 = (bf16[640,384]{1,0:T(8,128)(2,1)}, bf16[640,384]{1,0:T(8,128)(2,1)}, u32[]{:S(2)}, u32[]{:S(2)}) collective-permute-start(bf16[640,384]{1,0:T(8,128)(2,1)} %get-tuple-element.80), channel_id=1, source_target_pairs={{0,3},{1,0},{2,1},{3,2},{4,7},{5,4},{6,5},{7,6},{8,11},{9,8},{10,9... | collective-permute-start | bytes 1474568 | tf_op jit(solution)/shard_map/ppermute | solution.py:340
  145.1 2.6 %copy-start.23 = (bf16[192,640]{1,0:T(8,128)(2,1)S(1)}, bf16[192,640]{1,0:T(8,128)(2,1)}, u32[]{:S(2)}) copy-start(bf16[192,640]{1,0:T(8,128)(2,1)} %copy-done.22) | copy-start | bytes 737284
  145.1 2.6 %copy-start.25 = (bf16[192,640]{1,0:T(8,128)(2,1)S(1)}, bf16[192,640]{1,0:T(8,128)(2,1)}, u32[]{:S(2)}) copy-start(bf16[192,640]{1,0:T(8,128)(2,1)} %copy-done.24) | copy-start | bytes 737284
  145.2 2.6 %copy-start.27 = (bf16[192,640]{1,0:T(8,128)(2,1)S(1)}, bf16[192,640]{1,0:T(8,128)(2,1)}, u32[]{:S(2)}) copy-start(bf16[192,640]{1,0:T(8,128)(2,1)} %copy-done.26) | copy-start | bytes 737284
  145.2 2.5 %copy-start.29 = (bf16[192,640]{1,0:T(8,128)(2,1)S(1)}, bf16[192,640]{1,0:T(8,128)(2,1)}, u32[]{:S(2)}) copy-start(bf16[192,640]{1,0:T(8,128)(2,1)} %copy-done.28) | copy-start | bytes 737284
  146.8 0.9 copy-start.8
  147.7 5.2 %copy-start.16 = (bf16[256,384]{1,0:T(8,128)(2,1)S(1)}, bf16[256,384]{1,0:T(8,128)(2,1)}, u32[]{:S(2)}) copy-start(bf16[256,384]{1,0:T(8,128)(2,1)} %get-tuple-element.83.keep) | copy-start | bytes 589828
  152.9 20.1 %copy-start.2 = (bf16[2,1280,768]{2,1,0:T(8,128)(2,1)S(1)}, bf16[2,1280,768]{2,1,0:T(8,128)(2,1)}, u32[]{:S(2)}) copy-start(bf16[2,1280,768]{2,1,0:T(8,128)(2,1)} %copy-done) | copy-start | bytes 11796484
  156.2 47.4 %collective-permute-start.16 = (bf16[256,1280]{1,0:T(8,128)(2,1)S(1)}, bf16[256,1280]{1,0:T(8,128)(2,1)S(1)}, u32[]{:S(2)}, u32[]{:S(2)}) collective-permute-start(bf16[256,1280]{1,0:T(8,128)(2,1)S(1)} %get-tuple-element.89), channel_id=1, source_target_pairs={{0,4},{4,0},{1,5},{5,1},{2,6},{6,2},{3,7},{7,3},{8,12},{12,8},{9,1... | collective-permute-start | bytes 1966088 | tf_op jit(solution)/shard_map/ppermute | solution.py:356
  173.0 1.5 copy-start.15
  173.0 4.0 %copy-start.13 = (bf16[640,384]{1,0:T(8,128)(2,1)S(1)}, bf16[640,384]{1,0:T(8,128)(2,1)}, u32[]{:S(2)}) copy-start(bf16[640,384]{1,0:T(8,128)(2,1)} %copy-done.12) | copy-start | bytes 1474564
  175.7 40.7 %collective-permute-start.20 = (bf16[640,384]{1,0:T(8,128)(2,1)S(1)}, bf16[640,384]{1,0:T(8,128)(2,1)S(1)}, u32[]{:S(2)}, u32[]{:S(2)}) collective-permute-start(bf16[640,384]{1,0:T(8,128)(2,1)S(1)} %add_convert_fusion.1), channel_id=1, source_target_pairs={{0,3},{1,0},{2,1},{3,2},{4,7},{5,4},{6,5},{7,6},{8,11},{9,8},{10,9... | collective-permute-start | bytes 1474568 | tf_op jit(solution)/shard_map/ppermute | solution.py:358
  178.2 40.4 %collective-permute-start.18 = (bf16[640,384]{1,0:T(8,128)(2,1)S(1)}, bf16[640,384]{1,0:T(8,128)(2,1)S(1)}, u32[]{:S(2)}, u32[]{:S(2)}) collective-permute-start(bf16[640,384]{1,0:T(8,128)(2,1)S(1)} %add_convert_fusion.2), channel_id=1, source_target_pairs={{0,1},{1,2},{2,3},{3,0},{4,5},{5,6},{6,7},{7,4},{8,9},{9,10},{10,1... | collective-permute-start | bytes 1474568 | tf_op jit(solution)/shard_map/ppermute | solution.py:357
  203.8 17.0 %collective-permute-start.17 = (bf16[128,1280]{1,0:T(8,128)(2,1)S(1)}, bf16[128,1280]{1,0:T(8,128)(2,1)S(1)}, u32[]{:S(2)}, u32[]{:S(2)}) collective-permute-start(bf16[128,1280]{1,0:T(8,128)(2,1)S(1)} %slice.19), channel_id=1, source_target_pairs={{0,128},{128,0},{1,129},{129,1},{2,130},{130,2},{3,131},{131,3},{4... | collective-permute-start | bytes 983048 | tf_op jit(solution)/shard_map/ppermute | solution.py:365
